TPU v7x, 256 devices: a whole 4x4x8 slice. The times are simulated.
256 devices in a mesh: rows: 4 (over y_lo, core), shard: 64 (over x, y_hi, z).
Axes of the slice: x: 4, y: 4 (y_hi: 2, y_lo: 2; y = y_hi * 2 + y_lo), z: 8, core: 2. Of those that a mesh axis runs over, the one named last changes fastest.
Arguments:
- hidden_in: bfloat16 [128, 14336], P('rows', 'shard'), may hold values from -6 to 6
- resid: bfloat16 [128, 3584], P('rows'), may hold values from -6 to 6
- down_one: bfloat16 [14336, 3584], P('shard'), may hold values from -0.046875 to 0.046875
- gain_one: float32 [3584], replicated, may hold values from 0.5 to 1.5
- enc_weight: bfloat16 [3584, 65536], P(None, ('rows', 'shard')), may hold values from -0.09375 to 0.09375
- enc_bias: float32 [65536], P(('rows', 'shard')), may hold values from -3 to 3
- dec_weight: bfloat16 [65536, 3584], P(('rows', 'shard')), may hold values from -0.09375 to 0.09375
- dec_bias: float32 [3584], replicated, may hold values from -3 to 3
- gain_pre: float32 [3584], replicated, may hold values from 0.5 to 1.5
- gate_two: bfloat16 [3584, 14336], P(None, 'shard'), may hold values from -0.09375 to 0.09375
- up_two: bfloat16 [3584, 14336], P(None, 'shard'), may hold values from -0.09375 to 0.09375
- down_two: bfloat16 [14336, 3584], P('shard'), may hold values from -0.046875 to 0.046875
- gain_post: float32 [3584], replicated, may hold values from 0.5 to 1.5
Outputs:
- latents: bfloat16 [128, 65536], P(None, ('rows', 'shard'))
- delta: float32 [128, 3584], P('rows', 'shard')
All inputs are finite; a program needn't handle non-finite values.
Results may differ from a plain program's by a relative error of at most 0.0064.
Values may be sent and summed in bfloat16 or wider, within the bound.
A program may use at most 64 MiB of HBM per device.

v0:
```python
import jax
import jax.numpy as jnp
from jax import lax
from jax.sharding import PartitionSpec as P

D = 3584


def on_device(
    hidden_in,
    resid,
    down_one,
    gain_one,
    enc_weight,
    enc_bias,
    dec_weight,
    dec_bias,
    gain_pre,
    gate_two,
    up_two,
    down_two,
    gain_post,
):
    n_shard = lax.axis_size("shard")
    columns = D // n_shard
    offset = lax.axis_index("shard") * columns
    first_part = jnp.dot(hidden_in, down_one, preferred_element_type=jnp.float32)
    first = lax.psum(first_part, "shard")
    mean_sq = jnp.mean(first * first, axis=1, keepdims=True)
    clean = (resid.astype(jnp.float32) + first * lax.rsqrt(mean_sq + 1e-06) * gain_one).astype(
        jnp.bfloat16
    )
    clean_all = lax.all_gather(clean, "rows", axis=0, tiled=True)
    centered = (clean_all.astype(jnp.float32) - dec_bias).astype(jnp.bfloat16)
    pre_act = jnp.dot(centered, enc_weight, preferred_element_type=jnp.float32) + enc_bias
    latents = jnp.maximum(pre_act, 0.0).astype(jnp.bfloat16)
    group_sums = lax.psum_scatter(
        jnp.dot(latents, dec_weight, preferred_element_type=jnp.float32),
        "rows",
        scatter_dimension=0,
        tiled=True,
    )
    total = lax.psum(group_sums, "shard")
    recon = (total + dec_bias).astype(jnp.bfloat16)
    stream = jnp.concatenate([clean, recon], axis=0)
    upcast = stream.astype(jnp.float32)
    in_sq = jnp.mean(upcast * upcast, axis=1, keepdims=True)
    normed = (upcast * lax.rsqrt(in_sq + 1e-06) * gain_pre).astype(jnp.bfloat16)
    gate_out = jnp.dot(normed, gate_two, preferred_element_type=jnp.float32)
    up_out = jnp.dot(normed, up_two, preferred_element_type=jnp.float32)
    act = (jax.nn.gelu(gate_out, approximate=True) * up_out).astype(jnp.bfloat16)
    second_part = jnp.dot(act, down_two, preferred_element_type=jnp.float32)
    second_cols = lax.psum_scatter(second_part, "shard", scatter_dimension=1, tiled=True)
    second_sq = lax.psum(jnp.sum(second_cols * second_cols, axis=1), "shard")
    stream_cols = lax.dynamic_slice_in_dim(upcast, offset, columns, 1)
    post_cols = lax.dynamic_slice_in_dim(gain_post, offset, columns, 0)
    outputs = stream_cols + second_cols * lax.rsqrt(second_sq[:, None] / D + 1e-06) * post_cols
    half = clean.shape[0]
    delta = outputs[half:] - outputs[:half]
    return (latents, delta)


def solution(mesh):
    in_specs = (
        P("rows", "shard"),
        P("rows", None),
        P("shard", None),
        P(),
        P(None, ("rows", "shard")),
        P(("rows", "shard")),
        P(("rows", "shard"), None),
        P(),
        P(),
        P(None, "shard"),
        P(None, "shard"),
        P("shard", None),
        P(),
    )
    out_specs = (P(None, ("rows", "shard")), P("rows", "shard"))
    return jax.shard_map(
        on_device, mesh=mesh, in_specs=in_specs, out_specs=out_specs, check_vma=False
    )
```

profile of v0, /device:TPU:8, one launch (start us, length us, event | category | flops | bytes accessed | tf_op | source)
XLA Modules:
  0.0 2275.2 jit_solution(13110349626699264122)
XLA Ops:
  7.2 0.0 all-reduce.5.cloned.1.call-start
  7.2 2.7 fusion.22
  10.0 0.0 reduce-scatter.3.cloned.1.call-start
  10.1 678.9 %all-reduce.5.cloned.1.call-done = f32[32,3584]{1,0:T(8,128)} async-done(((f32[32,3584]{1,0:T(8,128)}), f32[32,3584]{1,0:T(8,128)}) %all-reduce.5.cloned.1.call-update) | async-done | bytes 458768 | tf_op jit(solution)/shard_map/psum | solution.py:28
  689.0 1.3 multiply_reduce_fusion.1
  690.3 1.2 add_convert_fusion.1
  691.5 8.9 all_gather.3
  700.4 0.4 fusion.1
  700.9 1.7 fusion.23
  702.6 0.0 all-reduce.7.cloned.1.call-start
  702.6 22.3 reduce-scatter.3.cloned.1.call-done
  725.0 680.6 %all-reduce.7.cloned.1.call-done = f32[32,3584]{1,0:T(8,128)} async-done(((f32[32,3584]{1,0:T(8,128)}), f32[32,3584]{1,0:T(8,128)}) %all-reduce.7.cloned.1.call-update) | async-done | bytes 458768 | tf_op jit(solution)/shard_map/psum | solution.py:43
  1405.6 1.0 add_convert_fusion
  1406.7 0.2 multiply_reduce_fusion
  1406.9 2.1 fusion.21
  1409.0 4.3 fusion.3
  1413.3 0.6 dynamic-slice
  1414.5 0.8 dynamic_slice.7
  1415.3 0.1 maximum_convert_fusion
  1415.3 672.4 %all-reduce.9.cloned.1.call-done = f32[64,3584]{1,0:T(8,128)} async-done(((f32[64,3584]{1,0:T(8,128)}), f32[64,3584]{1,0:T(8,128)}) %all-reduce.9.cloned.1.call-update) | async-done | bytes 917520
  2087.8 1.0 multiply_reduce_fusion.2
  2088.8 178.3 %psum.23 = f32[64]{0:T(128)S(1)} all-reduce(f32[64]{0:T(128)S(1)} %multiply_reduce_fusion.2), channel_id=1, replica_groups=mesh['rows'=4,'shard'=64] {'shard'}, use_global_device_ids=true, to_apply=%region_7.0 | all-reduce | flops 64 | bytes 512 | tf_op jit(solution)/shard_map/psum | solution.py:54
  2267.1 0.9 multiply_add_fusion
  2268.0 0.6 slice_subtract_fusion
  (26 shorter events, 0.2 us)
Async XLA Ops:
  7.2 693.7 %copy-start = (bf16[256,3584]{1,0:T(8,128)(2,1)S(1)}, bf16[256,3584]{1,0:T(8,128)(2,1)}, u32[]{:S(2)}) copy-start(bf16[256,3584]{1,0:T(8,128)(2,1)} %param.19) | copy-start | bytes 5505028
  7.2 683.1 %copy-start.1 = (bf16[32,3584]{1,0:T(8,128)(2,1)S(1)}, bf16[32,3584]{1,0:T(8,128)(2,1)}, u32[]{:S(2)}) copy-start(bf16[32,3584]{1,0:T(8,128)(2,1)} %param.14) | copy-start | bytes 688132
  7.2 683.1 %copy-start.3 = (f32[3584]{0:T(1024)S(1)}, f32[3584]{0:T(1024)}, u32[]{:S(2)}) copy-start(f32[3584]{0:T(1024)} %param.16) | copy-start | bytes 43012
  7.2 681.8 %all-reduce.5.cloned.1.call-start = ((), (), s32[]{:S(2)}) async-start(), calls=%async_computation.1 | async-start | bytes 917504 | tf_op jit(solution)/shard_map/psum | solution.py:28
  10.0 690.4 %copy-start.5 = (f32[3584]{0:T(1024)S(1)}, f32[3584]{0:T(1024)}, u32[]{:S(2)}) copy-start(f32[3584]{0:T(1024)} %param.20) | copy-start | bytes 43012
  10.0 690.4 %copy-start.7 = (f32[256]{0:T(256)S(1)}, f32[256]{0:T(256)}, u32[]{:S(2)}) copy-start(f32[256]{0:T(256)} %param.18) | copy-start | bytes 3076
  10.0 714.9 %reduce-scatter.3.cloned.1.call-start = ((), (), s32[]{:S(2)}) async-start(), calls=%async_computation.2 | async-start | bytes 2293760 | tf_op jit(solution)/shard_map/reduce_scatter | solution.py:37
  689.0 11.4 copy-start.6
  700.8 1.7 copy-start.2
  702.5 704.4 %copy-start.4 = (f32[3584]{0:T(1024)S(1)}, f32[3584]{0:T(1024)}, u32[]{:S(2)}) copy-start(f32[3584]{0:T(1024)} %param.21) | copy-start | bytes 43012
  702.6 703.1 %all-reduce.7.cloned.1.call-start = ((), (), s32[]{:S(2)}) async-start(), calls=%async_computation.3 | async-start | bytes 917504 | tf_op jit(solution)/shard_map/psum | solution.py:43
  725.0 1362.8 %all-reduce.9.cloned.1.call-start = ((), (), s32[]{:S(2)}) async-start(), calls=%async_computation.4 | async-start | bytes 1835008
  1408.9 4.3 copy-start.8
Sparse Core Ops, SparseCore 0:
  10.7 678.3 all-reduce.4
  702.7 22.2 reduce-scatter.2
  727.7 677.8 all-reduce.6
  1413.4 674.3 all-reduce.8
where the time goes:
time: 2280 us
  waiting for transfers between devices  2050 us (90%)
  blocking collectives  187 us (8%)
    psum x1, waiting for transfers between devices, on_device(): total = lax.psum(group_sums, 'shard')  681 us
    psum x1, waiting for transfers between devices, on_device(): first = lax.psum(first_part, 'shard')  679 us
    unnamed x5, waiting for transfers between devices  673 us
    psum x1, blocking collectives, on_device(): second_sq = lax.psum(jnp.sum(second_cols * second_cols, axis=1), 'shard')  178 us
  transfers between devices with their start and end apart: 4, of which 4 were waited for; matrix products, arithmetic and copies ran while one was open for 0% of the time, Pallas kernels for 0%

commit v1 on v0

v1 whole, which is shorter than its diff:
```python
import functools

import jax
import jax.numpy as jnp
from jax import lax
from jax.experimental import pallas as pl
from jax.experimental.pallas import tpu as pltpu
from jax.sharding import PartitionSpec as P

D = 3584
T = D // 128
MESH = pl.DeviceIdType.MESH
F32, BF16 = jnp.float32, jnp.bfloat16
EPS = 1e-06


def pick(ref, start, rows):
    tile, turn = start // 128, lax.rem(start, 128)
    lo = ref[0:rows, pl.ds(pl.multiple_of(tile * 128, 128), 128)]
    hi = ref[0:rows, pl.ds(pl.multiple_of(tile * 128 + 128, 128), 128)]
    shift = lax.rem(128 - turn, 128)
    lane = lax.broadcasted_iota(jnp.int32, (rows, 128), 1)
    return jnp.where(lane < 128 - turn, pltpu.roll(lo, shift, 1), pltpu.roll(hi, shift, 1))


def gelu(v):
    return 0.5 * v * (1.0 + jnp.tanh(0.7978845608028654 * (v + 0.044715 * (v * v * v))))


def kernel(
    hid_h, resid_h, d1_h, g1_h, enc_h, eb_h, dec_h, db_h, gpre_h, gate_h, up_h, d2_h, gpost_h,
    lat_o, delta_o,
    hid, resid, d1, g1, enc, eb, dec, db, gpre, gate, up, d2, gpost,
    parts, parts_b, land_b1, send_b2, land_b2, resid_c, g1_c, db_c, db_row, gpre_row, gpost_row,
    clean_all, cent, lhs, lat, pre_src, pre_land, e_src, e_own, land_e1, send_e2, land_e2, recon_p,
    clean_u, recon_u, lhs_f, f_src, f_own, land_f1, f_sum, send_f2, land_f2, second, send_f3, land_f3,
    load_sem, s_b1, r_b1, s_b2, r_b2, s_c, r_c, s_cc, r_cc, s_p, r_p, s_e1, r_e1, s_e2, r_e2, s_e3, r_e3,
    s_f1, r_f1, s_f2, r_f2, s_f3, r_f3,
):
    r = lax.axis_index("rows")
    s = lax.axis_index("shard")
    yl, c = r // 2, lax.rem(r, 2)
    k, z = s // 8, lax.rem(s, 8)
    x, yh = k // 2, lax.rem(k, 2)
    m = yl * 8 + k
    other = (yl * 2 + 1 - c, s)

    def in_k(i):
        return (r, lax.rem(k + i, 8) * 8 + z)

    def in_z(i):
        return (r, k * 8 + lax.rem(z + i, 8))

    def in_plane(i):
        to = lax.rem(m + i, 16)
        return ((to // 8) * 2 + c, lax.rem(to, 8) * 8 + z)

    def send(src, dst, s_sem, r_sem, device):
        return pltpu.make_async_remote_copy(
            src_ref=src, dst_ref=dst, send_sem=s_sem, recv_sem=r_sem, device_id=device, device_id_type=MESH
        )

    loads = [
        pltpu.make_async_copy(a, b, load_sem.at[i])
        for i, (a, b) in enumerate(
            (
                (hid_h, hid), (d1_h, d1), (resid_h, resid), (g1_h, g1), (db_h, db), (gpre_h, gpre), (gpost_h, gpost),
                (eb_h, eb), (enc_h, enc), (dec_h, dec), (gate_h, gate), (up_h, up), (d2_h, d2),
            )
        )
    ]
    for load in loads:
        load.start()

    barrier = pltpu.get_barrier_semaphore()

    @pl.loop(1, 16)
    def _(i):
        pl.semaphore_signal(barrier, inc=1, device_id=in_plane(i), device_id_type=MESH)

    @pl.loop(1, 8)
    def _(i):
        pl.semaphore_signal(barrier, inc=1, device_id=in_z(i), device_id_type=MESH)

    pl.semaphore_signal(barrier, inc=1, device_id=other, device_id_type=MESH)

    loads[0].wait()
    loads[1].wait()
    for g in range(7):
        part = jnp.dot(hid[...], d1[:, 512 * g : 512 * g + 512], preferred_element_type=F32)
        for j in range(4):
            row = 4 * (4 * g + j)
            for piece in range(8):
                parts[piece, row : row + 4, :] = part[4 * piece : 4 * piece + 4, 128 * j : 128 * j + 128]
    for piece in range(8):
        parts_b[piece] = parts[piece].astype(BF16)

    pl.semaphore_wait(barrier, 23)

    def b1(i):
        return send(parts_b.at[lax.rem(k + i, 8)], land_b1.at[i], s_b1.at[i], r_b1.at[i], in_k(i))

    @pl.loop(1, 8)
    def _(i):
        b1(i).start()

    for i in range(2, 8):
        loads[i].wait()
    for j in range(T):
        tile = slice(128 * j, 128 * j + 128)
        old = resid[:, tile].astype(F32)
        for piece in range(8):
            resid_c[piece, 4 * j : 4 * j + 4, :] = old[4 * piece : 4 * piece + 4, :]
        g1_c[4 * j : 4 * j + 4, :] = jnp.broadcast_to(g1[j : j + 1, :], (4, 128))
        db_c[4 * j : 4 * j + 4, :] = jnp.broadcast_to(db[j : j + 1, :], (4, 128))
        gpre_row[:, tile] = jnp.broadcast_to(gpre[j : j + 1, :], (8, 128))
        gpost_row[:, tile] = jnp.broadcast_to(gpost[j : j + 1, :], (8, 128))
        db_row[j // 7, :, 128 * (j % 7) : 128 * (j % 7) + 128] = jnp.broadcast_to(db[j : j + 1, :], (8, 128))
    gpost_row[:, D:] = jnp.zeros((8, 128), F32)
    clean_u[:, D:] = jnp.zeros((32, 128), F32)
    recon_u[:, D:] = jnp.zeros((32, 128), F32)
    second[:, :, 448:] = jnp.zeros((2, 32, 192), F32)
    f_src[:, :, :, 448:] = jnp.zeros((2, 8, 32, 64), BF16)
    f_own[:, :, :, 448:] = jnp.zeros((2, 8, 32, 64), F32)

    for i in range(1, 8):
        b1(i).wait_recv()
    total = parts[k]
    for i in range(1, 8):
        total += land_b1[i].astype(F32)
    send_b2[...] = total.astype(BF16)

    def b2(i):
        return send(send_b2, land_b2.at[i], s_b2.at[i], r_b2.at[i], in_z(i))

    @pl.loop(1, 8)
    def _(i):
        b2(i).start()

    for i in range(1, 8):
        b2(i).wait_recv()
    for i in range(1, 8):
        total += land_b2[i].astype(F32)
    squares = total[0:8] * total[0:8]
    for i in range(1, 14):
        squares += total[8 * i : 8 * i + 8] * total[8 * i : 8 * i + 8]
    squares += pltpu.roll(squares, 4, 0)
    scale = lax.rsqrt(jnp.sum(squares, axis=1, keepdims=True) / D + EPS)
    scale = jnp.concatenate([jnp.broadcast_to(scale, (8, 128))] * 14, axis=0)
    mine = r * 8 + k
    clean_all[mine] = (resid_c[k] + total * scale * g1_c[...]).astype(BF16)

    def spread(i):
        return send(clean_all.at[mine], clean_all.at[mine], s_c.at[i], r_c.at[i], in_plane(i))

    def arrival(i):
        source = lax.rem(m + 16 - i, 16)
        at = ((source // 8) * 2 + c) * 8 + lax.rem(source, 8)
        return send(clean_all.at[at], clean_all.at[at], s_c.at[i], r_c.at[i], in_plane(i)), at

    def forward(i, at):
        return send(clean_all.at[at], clean_all.at[at], s_cc.at[i], r_cc.at[i], other)

    @pl.loop(1, 16)
    def _(i):
        spread(i).start()

    forward(0, mine).start()

    @pl.loop(1, 16)
    def _(i):
        copy, at = arrival(i)
        copy.wait_recv()
        forward(i, at).start()

    @pl.loop(0, 16)
    def _(i):
        source = lax.rem(m + 16 - i, 16)
        at = ((source // 8) * 2 + 1 - c) * 8 + lax.rem(source, 8)
        forward(i, at).wait_recv()

    for q in range(32):
        centered = (clean_all[q].astype(F32) - db_c[...]).astype(BF16).astype(F32)
        for j in range(T):
            cent[4 * q : 4 * q + 4, 128 * j : 128 * j + 128] = centered[4 * j : 4 * j + 4, :]
    lhs[...] = cent[...].astype(BF16)
    loads[8].wait()
    pre_act = jnp.dot(lhs[...], enc[...], preferred_element_type=F32) + eb[...]
    lat[...] = jnp.maximum(pre_act, 0.0).astype(BF16)
    lat_o[...] = lat[...]

    def tokens_of(core):
        low = lat[pl.ds(pl.multiple_of(core * 32, 32), 32), :]
        high = lat[pl.ds(pl.multiple_of(core * 32 + 64, 32), 32), :]
        return jnp.concatenate([low, high], axis=0)

    def to_other(g):
        return send(pre_src.at[g], pre_land.at[g], s_p.at[g], r_p.at[g], other)

    loads[9].wait()
    theirs = tokens_of(1 - c)
    for g in range(4):
        cols = slice(896 * g, 896 * g + 896)
        pre_src[g] = jnp.dot(theirs, dec[:, cols], preferred_element_type=F32).astype(BF16)
        to_other(g).start()
    ours = tokens_of(c)

    def e1(g, to_yl, to_yh):
        to = to_yl * 8 + g * 2 + to_yh
        i = lax.rem(to + 16 - m, 16)
        row = 32 * to_yl + 16 * to_yh
        return to, send(e_src.at[g, row : row + 16, :], land_e1.at[i], s_e1.at[i], r_e1.at[i], in_plane(i))

    for g in range(4):
        cols = slice(896 * g, 896 * g + 896)
        e_own[g] = jnp.dot(ours, dec[:, cols], preferred_element_type=F32)
        to_other(g).wait_recv()
        e_own[g] += pre_land[g].astype(F32)
        e_src[g] = e_own[g].astype(BF16)
        for to_yl in range(2):
            for to_yh in range(2):
                to, copy = e1(g, to_yl, to_yh)

                @pl.when(to != m)
                def _(copy=copy):
                    copy.start()

    def layer(h, stream):
        squares = jnp.zeros((32, 128), F32)
        for j in range(T):
            tile = stream[:, 128 * j : 128 * j + 128]
            squares += tile * tile
        scale = lax.rsqrt(jnp.sum(squares, axis=1, keepdims=True) / D + EPS)
        for g in range(7):
            cols = slice(512 * g, 512 * g + 512)
            lhs_f[h, :, cols] = (stream[:, cols] * scale * gpre_row[0:1, cols]).astype(BF16)
        gate_out = jnp.dot(lhs_f[h], gate[...], preferred_element_type=F32)
        up_out = jnp.dot(lhs_f[h], up[...], preferred_element_type=F32)
        act = (gelu(gate_out) * up_out).astype(BF16)
        for g in range(4):
            part = jnp.dot(act, d2[:, 896 * g : 896 * g + 896], preferred_element_type=F32)
            for half in range(2):
                piece = part[:, 448 * half : 448 * half + 448]
                f_own[h, 2 * g + half, :, 0:448] = piece
                f_src[h, 2 * g + half, :, 0:448] = piece.astype(BF16)

    for q in range(8):
        clean = clean_all[r * 8 + q].astype(F32)
        for j in range(T):
            clean_u[4 * q : 4 * q + 4, 128 * j : 128 * j + 128] = clean[4 * j : 4 * j + 4, :]
    loads[10].wait()
    loads[11].wait()
    loads[12].wait()
    layer(0, clean_u)

    for i in range(1, 16):
        send(land_e1.at[i], land_e1.at[i], s_e1.at[i], r_e1.at[i], in_plane(i)).wait_recv()
    row = pl.multiple_of(32 * yl + 16 * yh, 16)
    total = e_own[x, pl.ds(row, 16), :]
    for i in range(1, 16):
        total += land_e1[i].astype(F32)
    send_e2[...] = total.astype(BF16)

    def e2(i):
        return send(send_e2, land_e2.at[i], s_e2.at[i], r_e2.at[i], in_z(i))

    @pl.loop(1, 8)
    def _(i):
        e2(i).start()

    def f1(h, i):
        return send(f_src.at[h, lax.rem(k + i, 8)], land_f1.at[h, i], s_f1.at[h, i], r_f1.at[h, i], in_k(i))

    def f2(h, i):
        return send(send_f2.at[h], land_f2.at[h, i], s_f2.at[h, i], r_f2.at[h, i], in_z(i))

    def f3(h, i):
        return send(send_f3.at[h], land_f3.at[h, i], s_f3.at[h, i], r_f3.at[h, i], in_k(i))

    @pl.loop(1, 8)
    def _(i):
        f1(0, i).start()

    for i in range(1, 8):
        e2(i).wait_recv()
    for i in range(1, 8):
        total += land_e2[i].astype(F32)
    recon_p[k] = (total + db_row[x, 0:1, :]).astype(BF16)

    def e3(i):
        return send(recon_p.at[k], recon_p.at[k], s_e3.at[i], r_e3.at[i], in_k(i))

    @pl.loop(1, 8)
    def _(i):
        e3(i).start()

    def sum_over_k(h):
        for i in range(1, 8):
            f1(h, i).wait_recv()
        total = f_own[h, k]
        for i in range(1, 8):
            total += land_f1[h, i].astype(F32)
        f_sum[h] = total
        send_f2[h] = total.astype(BF16)

        @pl.loop(1, 8)
        def _(i):
            f2(h, i).start()

    diagonal = (
        lax.broadcasted_iota(jnp.int32, (32, 128), 0) == lax.broadcasted_iota(jnp.int32, (32, 128), 1)
    ).astype(F32)

    def sum_over_z(h):
        for i in range(1, 8):
            f2(h, i).wait_recv()
        total = f_sum[h]
        for i in range(1, 8):
            total += land_f2[h, i].astype(F32)
        second[h, :, 0:512] = total
        squares = jnp.sum(total * total, axis=1, keepdims=True)
        flat = jnp.sum(squares * diagonal, axis=0, keepdims=True)
        send_f3[h] = jnp.broadcast_to(flat, (8, 128))

        @pl.loop(1, 8)
        def _(i):
            f3(h, i).start()

    def outputs(h, stream):
        for i in range(1, 8):
            f3(h, i).wait_recv()
        flat = send_f3[h]
        for i in range(1, 8):
            flat += land_f3[h, i]
        squares = jnp.sum(flat[0:1, :] * diagonal, axis=1, keepdims=True)
        gain = pick(gpost_row, 56 * s, 8)[0:1, :]
        return pick(stream, 56 * s, 32) + pick(second.at[h], 56 * z, 32) * lax.rsqrt(squares / D + EPS) * gain

    sum_over_k(0)

    def arrived(i):
        at = lax.rem(k + 8 - i, 8)
        return send(recon_p.at[at], recon_p.at[at], s_e3.at[i], r_e3.at[i], in_k(i))

    for i in range(1, 8):
        arrived(i).wait_recv()
    for q in range(8):
        row, col = 16 * (q % 2), 896 * (q // 2)
        recon_u[row : row + 16, col : col + 896] = recon_p[q].astype(F32)
    layer(1, recon_u)

    @pl.loop(1, 8)
    def _(i):
        f1(1, i).start()

    sum_over_z(0)
    sum_over_k(1)
    clean_out = outputs(0, clean_u)
    sum_over_z(1)
    delta_o[...] = outputs(1, recon_u) - clean_out

    @pl.loop(1, 8)
    def _(i):
        b1(i).wait_send()
        b2(i).wait_send()
        e2(i).wait_send()
        e3(i).wait_send()
        for h in range(2):
            f1(h, i).wait_send()
            f2(h, i).wait_send()
            f3(h, i).wait_send()

    @pl.loop(1, 16)
    def _(i):
        spread(i).wait_send()
        send(land_e1.at[i], land_e1.at[i], s_e1.at[i], r_e1.at[i], in_plane(i)).wait_send()

    @pl.loop(0, 16)
    def _(i):
        forward(i, mine).wait_send()

    for g in range(4):
        to_other(g).wait_send()


def on_device(
    hidden_in, resid, down_one, gain_one, enc_weight, enc_bias, dec_weight, dec_bias, gain_pre, gate_two, up_two,
    down_two, gain_post,
):
    tiles = (T, 128)
    args = (
        hidden_in, resid, down_one, gain_one.reshape(tiles), enc_weight, enc_bias.reshape(1, 256), dec_weight,
        dec_bias.reshape(tiles), gain_pre.reshape(tiles), gate_two, up_two, down_two, gain_post.reshape(tiles),
    )
    dma = pltpu.SemaphoreType.DMA
    vmem = pltpu.VMEM
    latents, delta = pl.pallas_call(
        kernel,
        name="spliced",
        out_shape=(jax.ShapeDtypeStruct((128, 256), BF16), jax.ShapeDtypeStruct((32, 128), F32)),
        in_specs=[pl.BlockSpec(memory_space=pl.ANY)] * len(args),
        out_specs=[pl.BlockSpec(memory_space=pltpu.VMEM)] * 2,
        scratch_shapes=[vmem(a.shape, a.dtype) for a in args]
        + [
            vmem((8, 112, 128), F32),
            vmem((8, 112, 128), BF16),
            vmem((8, 112, 128), BF16),
            vmem((112, 128), BF16),
            vmem((8, 112, 128), BF16),
            vmem((8, 112, 128), F32),
            vmem((112, 128), F32),
            vmem((112, 128), F32),
            vmem((4, 8, 896), F32),
            vmem((8, D), F32),
            vmem((8, D + 128), F32),
            vmem((32, 112, 128), BF16),
            vmem((128, D), F32),
            vmem((128, D), BF16),
            vmem((128, 256), BF16),
            vmem((4, 64, 896), BF16),
            vmem((4, 64, 896), BF16),
            vmem((4, 64, 896), BF16),
            vmem((4, 64, 896), F32),
            vmem((16, 16, 896), BF16),
            vmem((16, 896), BF16),
            vmem((8, 16, 896), BF16),
            vmem((8, 16, 896), BF16),
            vmem((32, D + 128), F32),
            vmem((32, D + 128), F32),
            vmem((2, 32, D), BF16),
            vmem((2, 8, 32, 512), BF16),
            vmem((2, 8, 32, 512), F32),
            vmem((2, 8, 32, 512), BF16),
            vmem((2, 32, 512), F32),
            vmem((2, 32, 512), BF16),
            vmem((2, 8, 32, 512), BF16),
            vmem((2, 32, 640), F32),
            vmem((2, 8, 128), F32),
            vmem((2, 8, 8, 128), F32),
            dma((13,)),
            dma((8,)), dma((8,)), dma((8,)), dma((8,)),
            dma((16,)), dma((16,)), dma((16,)), dma((16,)),
            dma((4,)), dma((4,)), dma((16,)), dma((16,)),
            dma((8,)), dma((8,)), dma((8,)), dma((8,)),
            dma((2, 8)), dma((2, 8)), dma((2, 8)), dma((2, 8)), dma((2, 8)), dma((2, 8)),
        ],
        compiler_params=pltpu.CompilerParams(
            collective_id=0, has_side_effects=True, vmem_limit_bytes=48 * 2**20
        ),
        cost_estimate=pl.CostEstimate(flops=10**9, bytes_accessed=12 * 10**6, transcendentals=10**5),
    )(*args)
    return latents, delta[:, :56]


def solution(mesh):
    in_specs = (
        P("rows", "shard"),
        P("rows", None),
        P("shard", None),
        P(),
        P(None, ("rows", "shard")),
        P(("rows", "shard")),
        P(("rows", "shard"), None),
        P(),
        P(),
        P(None, "shard"),
        P(None, "shard"),
        P("shard", None),
        P(),
    )
    out_specs = (P(None, ("rows", "shard")), P("rows", "shard"))
    return jax.shard_map(on_device, mesh=mesh, in_specs=in_specs, out_specs=out_specs, check_vma=False)
```

time: 2280 us -> 90.4 us (0.04)
  waiting for transfers between devices: 2050 us -> 0 us
  blocking collectives: 187 us -> 0 us
  Pallas kernels: 0 us -> 78.2 us
    psum x2 -> x0, waiting for transfers between devices: 1360 us -> none  [the longest x1 681 us: on_device(): total = lax.psum(group_sums, 'shard')]
    unnamed x5 -> x0, waiting for transfers between devices: 673 us -> none
    psum x1 -> x0, blocking collectives: 178 us -> none  [on_device(): second_sq = lax.psum(jnp.sum(second_cols * second_cols, axis=1), 'shard')]
    pallas_call x0 -> x1, Pallas kernels: none -> 78.2 us  [on_device(): pl.pallas_call(kernel, name='spliced', out_shape=(jax.ShapeDtypeStruct((1...]
  transfers between devices with their start and end apart: 4 -> 0, of which waited for: 4 -> 0; matrix products, arithmetic and copies ran while one was open for 0% -> 0% of each run, Pallas kernels for 0% -> 0%
where the time goes in v1:
time: 90.4 us; the launch traced here: 90.2 us
  Pallas kernels  78.2 us (87%)
  local copies, waits for them, and re-layouts  11.2 us (12%)
    pallas_call x1, Pallas kernels, on_device(): pl.pallas_call(kernel, name='spliced', out_shape=(jax.ShapeDtypeStruct((1...  78.2 us
    unnamed x24, local copies, waits for them, and re-layouts  11.2 us

profile of v1, /device:TPU:8, one launch (start us, length us, event | category | flops | bytes accessed | tf_op | source)
XLA Modules:
  0.0 90.2 jit_solution(14350642904834041398)
XLA Ops:
  0.6 0.0 copy-start.4
  0.6 0.0 copy-start.5
  0.7 0.0 copy-start.6
  0.7 0.0 copy-start.7
  0.7 0.0 copy-start.8
  0.7 0.0 copy-start.9
  0.7 3.8 %copy.15.gate_h = bf16[3584,224]{1,0:T(8,128)(2,1)} copy(bf16[3584,224]{0,1:T(8,128)(2,1)} %param.22) | data formatting | bytes 3211264 | tf_op args[9]
  4.4 0.0 copy-start
  4.4 0.0 copy-start.1
  4.4 3.9 %copy.16.up_h = bf16[3584,224]{1,0:T(8,128)(2,1)} copy(bf16[3584,224]{0,1:T(8,128)(2,1)} %param.23) | data formatting | bytes 3211264 | tf_op args[10]
  8.3 0.0 copy-done.4
  8.3 0.0 copy-done.5
  8.3 0.0 copy-done.6
  8.3 0.0 copy-done.7
  8.3 0.0 copy-done.8
  8.3 0.0 copy-done.9
  8.4 0.0 copy-done
  8.4 0.0 copy-done.1
  8.4 0.0 copy-start.2
  8.4 1.4 %copy-done.2 = bf16[224,3584]{1,0:T(8,128)(2,1)S(1)} copy-done((bf16[224,3584]{1,0:T(8,128)(2,1)S(1)}, bf16[224,3584]{1,0:T(8,128)(2,1)}, u32[]{:S(2)}) %copy-start.2) | copy-done | bytes 1605656
  9.8 0.9 %copy-done.3 = bf16[32,3584]{1,0:T(8,128)(2,1)S(1)} copy-done((bf16[32,3584]{1,0:T(8,128)(2,1)S(1)}, bf16[32,3584]{1,0:T(8,128)(2,1)}, u32[]{:S(2)}) %copy-start.3) | copy-done | bytes 229400
  10.7 78.2 %spliced.1 = (bf16[128,256]{1,0:T(8,128)(2,1)S(1)}, f32[32,128]{1,0:T(8,128)S(1)}) custom-call(bf16[32,224]{1,0:T(8,128)(2,1)S(1)} %copy-done.4, bf16[32,3584]{1,0:T(8,128)(2,1)S(1)} %copy-done.3, bf16[224,3584]{1,0:T(8,128)(2,1)S(1)} %copy-done.1, f32[28,128]{1,0:T(8,128)S(1)} %bitcast.6, bf16[3584,256]{1,0:T(8,128)(2,1)S(1)} %copy-done, ...), custom_call_target="tpu_custom_call" | custom-call | flops 1000000000 | bytes 12000000 | tf_op jit(solution)/shard_map/spliced/pallas_call | solution.py:397
  88.9 0.6 copy.19
  89.6 0.6 copy.20
  (1 shorter events, 0.0 us)
Async XLA Ops:
  0.6 7.7 %copy-start.4 = (bf16[32,224]{1,0:T(8,128)(2,1)S(1)}, bf16[32,224]{1,0:T(8,128)(2,1)}, u32[]{:S(2)}) copy-start(bf16[32,224]{1,0:T(8,128)(2,1)} %hid_h.1) | copy-start | bytes 43012
  0.6 7.7 %copy-start.5 = (f32[3584]{0:T(1024)S(1)}, f32[3584]{0:T(1024)}, u32[]{:S(2)}) copy-start(f32[3584]{0:T(1024)} %param.16) | copy-start | bytes 43012
  0.7 7.7 %copy-start.6 = (f32[3584]{0:T(1024)S(1)}, f32[3584]{0:T(1024)}, u32[]{:S(2)}) copy-start(f32[3584]{0:T(1024)} %param.20) | copy-start | bytes 43012
  0.7 7.7 %copy-start.7 = (f32[3584]{0:T(1024)S(1)}, f32[3584]{0:T(1024)}, u32[]{:S(2)}) copy-start(f32[3584]{0:T(1024)} %param.21) | copy-start | bytes 43012
  0.7 7.7 %copy-start.8 = (f32[3584]{0:T(1024)S(1)}, f32[3584]{0:T(1024)}, u32[]{:S(2)}) copy-start(f32[3584]{0:T(1024)} %param.25) | copy-start | bytes 43012
  0.7 7.7 %copy-start.9 = (f32[256]{0:T(256)S(1)}, f32[256]{0:T(256)}, u32[]{:S(2)}) copy-start(f32[256]{0:T(256)} %param.18) | copy-start | bytes 3076
  4.4 3.9 %copy-start = (bf16[3584,256]{1,0:T(8,128)(2,1)S(1)}, bf16[3584,256]{1,0:T(8,128)(2,1)}, u32[]{:S(2)}) copy-start(bf16[3584,256]{1,0:T(8,128)(2,1)} %enc_h.1) | copy-start | bytes 5505028
  4.4 3.9 %copy-start.1 = (bf16[224,3584]{1,0:T(8,128)(2,1)S(1)}, bf16[224,3584]{1,0:T(8,128)(2,1)}, u32[]{:S(2)}) copy-start(bf16[224,3584]{1,0:T(8,128)(2,1)} %d1_h.1) | copy-start | bytes 4816900
  8.4 1.4 %copy-start.2 = (bf16[224,3584]{1,0:T(8,128)(2,1)S(1)}, bf16[224,3584]{1,0:T(8,128)(2,1)}, u32[]{:S(2)}) copy-start(bf16[224,3584]{1,0:T(8,128)(2,1)} %d2_h.1) | copy-start | bytes 4816900
  9.8 0.9 %copy-start.3 = (bf16[32,3584]{1,0:T(8,128)(2,1)S(1)}, bf16[32,3584]{1,0:T(8,128)(2,1)}, u32[]{:S(2)}) copy-start(bf16[32,3584]{1,0:T(8,128)(2,1)} %resid_h.1) | copy-start | bytes 688132

commit v2 on v1

--- a/solution.py
+++ b/solution.py
@@ -234,8 +234,8 @@
         for g in range(7):
             cols = slice(512 * g, 512 * g + 512)
             lhs_f[h, :, cols] = (stream[:, cols] * scale * gpre_row[0:1, cols]).astype(BF16)
-        gate_out = jnp.dot(lhs_f[h], gate[...], preferred_element_type=F32)
-        up_out = jnp.dot(lhs_f[h], up[...], preferred_element_type=F32)
+        gate_out = lax.dot_general(lhs_f[h], gate[...], (((1,), (1,)), ((), ())), preferred_element_type=F32)
+        up_out = lax.dot_general(lhs_f[h], up[...], (((1,), (1,)), ((), ())), preferred_element_type=F32)
         act = (gelu(gate_out) * up_out).astype(BF16)
         for g in range(4):
             part = jnp.dot(act, d2[:, 896 * g : 896 * g + 896], preferred_element_type=F32)
@@ -390,14 +390,15 @@
     tiles = (T, 128)
     args = (
         hidden_in, resid, down_one, gain_one.reshape(tiles), enc_weight, enc_bias.reshape(1, 256), dec_weight,
-        dec_bias.reshape(tiles), gain_pre.reshape(tiles), gate_two, up_two, down_two, gain_post.reshape(tiles),
+        dec_bias.reshape(tiles), gain_pre.reshape(tiles), gate_two.T, up_two.T, down_two,
+        gain_post.reshape(tiles),
     )
     dma = pltpu.SemaphoreType.DMA
     vmem = pltpu.VMEM
     latents, delta = pl.pallas_call(
         kernel,
         name="spliced",
-        out_shape=(jax.ShapeDtypeStruct((128, 256), BF16), jax.ShapeDtypeStruct((32, 128), F32)),
+        out_shape=(vmem((128, 256), BF16), vmem((32, 128), F32)),
         in_specs=[pl.BlockSpec(memory_space=pl.ANY)] * len(args),
         out_specs=[pl.BlockSpec(memory_space=pltpu.VMEM)] * 2,
         scratch_shapes=[vmem(a.shape, a.dtype) for a in args]
@@ -445,7 +446,7 @@
             dma((2, 8)), dma((2, 8)), dma((2, 8)), dma((2, 8)), dma((2, 8)), dma((2, 8)),
         ],
         compiler_params=pltpu.CompilerParams(
-            collective_id=0, has_side_effects=True, vmem_limit_bytes=48 * 2**20
+            collective_id=0, has_side_effects=True, vmem_limit_bytes=62 * 2**20
         ),
         cost_estimate=pl.CostEstimate(flops=10**9, bytes_accessed=12 * 10**6, transcendentals=10**5),
     )(*args)

time: 90.4 us -> 80 us (0.88)
  local copies, waits for them, and re-layouts: 11.2 us -> 1.24 us
    unnamed x24 -> x2, local copies, waits for them, and re-layouts: 11.2 us -> 1.24 us
where the time goes in v2:
time: 80 us; the launch traced here: 79.8 us
  Pallas kernels  77.9 us (97%)
  local copies, waits for them, and re-layouts  1.24 us (2%)
    pallas_call x1, Pallas kernels, on_device(): pl.pallas_call(kernel, name='spliced', out_shape=(vmem((128, 256), BF16),...  77.9 us

profile of v2, /device:TPU:8, one launch (start us, length us, event | category | flops | bytes accessed | tf_op | source)
XLA Modules:
  0.0 79.8 jit_solution(2824045976712963225)
XLA Ops:
  0.6 77.9 %spliced.1 = (bf16[128,256]{1,0:T(8,128)(2,1)S(1)}, f32[32,128]{1,0:T(8,128)S(1)}) custom-call(bf16[32,224]{1,0:T(8,128)(2,1)} %hid_h.1, bf16[32,3584]{1,0:T(8,128)(2,1)} %resid_h.1, bf16[224,3584]{1,0:T(8,128)(2,1)} %d1_h.1, f32[28,128]{1,0:T(8,128)} %bitcast.11, bf16[3584,256]{1,0:T(8,128)(2,1)} %enc_h.1, f32[1,256]{1,0:T(1,128)} %bitcast.15, ...), custom_call_target="tpu_custom_call" | custom-call | flops 1000000000 | bytes 12000000 | tf_op jit(solution)/shard_map/spliced/pallas_call | solution.py:398
  78.5 0.6 copy.17
  79.2 0.6 copy.18

commit v3 on v2

v3 whole, which is shorter than its diff:
```python
import functools

import jax
import jax.numpy as jnp
from jax import lax
from jax.experimental import pallas as pl
from jax.experimental.pallas import tpu as pltpu
from jax.sharding import PartitionSpec as P

D = 3584
T = D // 128
MESH = pl.DeviceIdType.MESH
F32, BF16 = jnp.float32, jnp.bfloat16
EPS = 1e-06


def pick(ref, start, rows):
    tile, turn = start // 128, lax.rem(start, 128)
    lo = ref[0:rows, pl.ds(pl.multiple_of(tile * 128, 128), 128)]
    hi = ref[0:rows, pl.ds(pl.multiple_of(tile * 128 + 128, 128), 128)]
    shift = lax.rem(128 - turn, 128)
    lane = lax.broadcasted_iota(jnp.int32, (rows, 128), 1)
    return jnp.where(lane < 128 - turn, pltpu.roll(lo, shift, 1), pltpu.roll(hi, shift, 1))


def around(t, n):
    return lax.rem(n // 2 + n + (1 - 2 * lax.rem(t, 2)) * ((t + 1) // 2), n)


def gelu(v):
    return 0.5 * v * (1.0 + jnp.tanh(0.7978845608028654 * (v + 0.044715 * (v * v * v))))


def kernel(
    hid_h, resid_h, d1_h, g1_h, enc_h, eb_h, dec_h, db_h, gpre_h, gate_h, up_h, d2_h, gpost_h,
    lat_o, delta_o,
    hid, resid, d1, g1, enc, eb, dec, db, gpre, gate, up, d2, gpost,
    parts, parts_b, land_b1, send_b2, land_b2, resid_c, g1_c, db_c, db_row, gpre_row, gpost_row,
    clean_all, cent, lhs, lat, pre_src, pre_land, e_src, e_own, land_e1, send_e2, land_e2, recon_p,
    clean_u, recon_u, lhs_f, f_src, f_own, land_f1, f_sum, send_f2, land_f2, second, send_f3, land_f3,
    load_sem, s_b1, r_b1, s_b2, r_b2, s_c, r_c, s_cc, r_cc, s_p, r_p, s_e1, r_e1, s_e2, r_e2, s_e3, r_e3,
    s_f1, r_f1, s_f2, r_f2, s_f3, r_f3,
):
    r = lax.axis_index("rows")
    s = lax.axis_index("shard")
    yl, c = r // 2, lax.rem(r, 2)
    k, z = s // 8, lax.rem(s, 8)
    x, yh = k // 2, lax.rem(k, 2)
    y = 2 * yh + yl
    other = (yl * 2 + 1 - c, s)

    def k_at(t):
        return lax.rem(x + around(t // 2, 4), 4) * 2 + lax.rem(yh + 1 - lax.rem(t, 2), 2)

    def k_from(t):
        return lax.rem(x + 4 - around(t // 2, 4), 4) * 2 + lax.rem(yh + 1 - lax.rem(t, 2), 2)

    def in_k(t):
        return (r, k_at(t) * 8 + z)

    def in_z(t):
        return (r, k * 8 + lax.rem(z + around(t, 8), 8))

    def plane_at(to_x, to_y):
        return (lax.rem(to_y, 2) * 2 + c, (to_x * 2 + to_y // 2) * 8 + z)

    def in_plane(t):
        return plane_at(lax.rem(x + around(t // 4, 4), 4), lax.rem(y + around(lax.rem(t, 4), 4), 4))

    def chunk_from(t, core):
        from_x = lax.rem(x + 4 - around(t // 4, 4), 4)
        from_y = lax.rem(y + 4 - around(lax.rem(t, 4), 4), 4)
        return (lax.rem(from_y, 2) * 2 + core) * 8 + from_x * 2 + from_y // 2

    def send(src, dst, s_sem, r_sem, device):
        return pltpu.make_async_remote_copy(
            src_ref=src, dst_ref=dst, send_sem=s_sem, recv_sem=r_sem, device_id=device, device_id_type=MESH
        )

    loads = [
        pltpu.make_async_copy(a, b, load_sem.at[i])
        for i, (a, b) in enumerate(
            (
                (hid_h, hid), (d1_h, d1), (resid_h, resid), (g1_h, g1), (db_h, db), (gpre_h, gpre), (gpost_h, gpost),
                (eb_h, eb), (enc_h, enc), (dec_h, dec), (gate_h, gate), (up_h, up), (d2_h, d2),
            )
        )
    ]
    for load in loads:
        load.start()

    barrier = pltpu.get_barrier_semaphore()

    @pl.loop(0, 15)
    def _(t):
        pl.semaphore_signal(barrier, inc=1, device_id=in_plane(t), device_id_type=MESH)

    @pl.loop(0, 7)
    def _(t):
        pl.semaphore_signal(barrier, inc=1, device_id=in_z(t), device_id_type=MESH)

    pl.semaphore_signal(barrier, inc=1, device_id=other, device_id_type=MESH)

    loads[0].wait()
    loads[1].wait()
    for g in range(7):
        part = jnp.dot(hid[...], d1[:, 512 * g : 512 * g + 512], preferred_element_type=F32)
        for j in range(4):
            row = 4 * (4 * g + j)
            for piece in range(8):
                parts[piece, row : row + 4, :] = part[4 * piece : 4 * piece + 4, 128 * j : 128 * j + 128]
    for piece in range(8):
        parts_b[piece] = parts[piece].astype(BF16)

    pl.semaphore_wait(barrier, 23)

    halves = ((0, 64), (64, 48))

    def b1(h, t):
        rows = pl.ds(*halves[h])
        return send(
            parts_b.at[k_at(t), rows, :], land_b1.at[t, rows, :], s_b1.at[h, t], r_b1.at[h, t], in_k(t)
        )

    for h in range(2):

        @pl.loop(0, 7)
        def _(t, h=h):
            b1(h, t).start()

    for i in range(2, 8):
        loads[i].wait()
    for j in range(T):
        tile = slice(128 * j, 128 * j + 128)
        old = resid[:, tile].astype(F32)
        for piece in range(8):
            resid_c[piece, 4 * j : 4 * j + 4, :] = old[4 * piece : 4 * piece + 4, :]
        g1_c[4 * j : 4 * j + 4, :] = jnp.broadcast_to(g1[j : j + 1, :], (4, 128))
        db_c[4 * j : 4 * j + 4, :] = jnp.broadcast_to(db[j : j + 1, :], (4, 128))
        gpre_row[:, tile] = jnp.broadcast_to(gpre[j : j + 1, :], (8, 128))
        gpost_row[:, tile] = jnp.broadcast_to(gpost[j : j + 1, :], (8, 128))
        db_row[j // 7, :, 128 * (j % 7) : 128 * (j % 7) + 128] = jnp.broadcast_to(db[j : j + 1, :], (8, 128))
    gpost_row[:, D:] = jnp.zeros((8, 128), F32)
    clean_u[:, D:] = jnp.zeros((32, 128), F32)
    recon_u[:, D:] = jnp.zeros((32, 128), F32)
    second[:, :, 448:] = jnp.zeros((2, 32, 192), F32)
    f_src[:, :, :, 448:] = jnp.zeros((2, 8, 32, 64), BF16)
    f_own[:, :, :, 448:] = jnp.zeros((2, 8, 32, 64), F32)

    def b2(h, t):
        rows = pl.ds(*halves[h])
        return send(send_b2.at[rows, :], land_b2.at[t, rows, :], s_b2.at[h, t], r_b2.at[h, t], in_z(t))

    sums = []
    for h, (low, count) in enumerate(halves):
        for t in range(7):
            b1(h, t).wait_recv()
        total = parts[k, low : low + count, :]
        for t in range(7):
            total += land_b1[t, low : low + count, :].astype(F32)
        send_b2[low : low + count, :] = total.astype(BF16)

        @pl.loop(0, 7)
        def _(t, h=h):
            b2(h, t).start()

        sums.append(total)

    for h, (low, count) in enumerate(halves):
        for t in range(7):
            b2(h, t).wait_recv()
        for t in range(7):
            sums[h] += land_b2[t, low : low + count, :].astype(F32)
    total = jnp.concatenate(sums, axis=0)
    squares = total[0:8] * total[0:8]
    for i in range(1, 14):
        squares += total[8 * i : 8 * i + 8] * total[8 * i : 8 * i + 8]
    squares += pltpu.roll(squares, 4, 0)
    scale = lax.rsqrt(jnp.sum(squares, axis=1, keepdims=True) / D + EPS)
    scale = jnp.concatenate([jnp.broadcast_to(scale, (8, 128))] * 14, axis=0)
    mine = r * 8 + k
    clean_all[mine] = (resid_c[k] + total * scale * g1_c[...]).astype(BF16)

    def spread(t):
        return send(clean_all.at[mine], clean_all.at[mine], s_c.at[t], r_c.at[t], in_plane(t))

    def forward(t, at):
        return send(clean_all.at[at], clean_all.at[at], s_cc.at[t], r_cc.at[t], other)

    def place(core):
        @pl.loop(0, 2)
        def _(low):
            group = low * 2 + core
            for q in range(8):
                centered = (clean_all[group * 8 + q].astype(F32) - db_c[...]).astype(BF16).astype(F32)
                for j in range(T):
                    cent[group, 4 * q : 4 * q + 4, 128 * j : 128 * j + 128] = centered[4 * j : 4 * j + 4, :]
            lhs[pl.ds(pl.multiple_of(group * 32, 32), 32), :] = cent[group].astype(BF16)

    @pl.loop(0, 15)
    def _(t):
        spread(t).start()

    forward(15, mine).start()

    @pl.loop(0, 15)
    def _(i):
        t = 14 - i
        at = chunk_from(t, c)
        send(clean_all.at[at], clean_all.at[at], s_c.at[t], r_c.at[t], in_plane(t)).wait_recv()
        forward(t, at).start()

    place(c)

    @pl.loop(0, 16)
    def _(i):
        t = 15 - i
        at = chunk_from(t, 1 - c)
        forward(t, at).wait_recv()

    place(1 - c)
    loads[8].wait()
    pre_act = jnp.dot(lhs[...], enc[...], preferred_element_type=F32) + eb[...]
    lat[...] = jnp.maximum(pre_act, 0.0).astype(BF16)
    lat_o[...] = lat[...]

    cuts = ((0, 512), (512, 384))

    def tokens_of(core):
        low = lat[pl.ds(pl.multiple_of(core * 32, 32), 32), :]
        high = lat[pl.ds(pl.multiple_of(core * 32 + 64, 32), 32), :]
        return jnp.concatenate([low, high], axis=0)

    def decoded(tokens, g, h):
        first_col = lax.rem(x + around(jnp.int32(g), 4), 4) * 896 + cuts[h][0]
        cols = pl.ds(pl.multiple_of(first_col, 128), cuts[h][1])
        return jnp.dot(tokens, dec[:, cols], preferred_element_type=F32)

    def to_other(h, g):
        cols = pl.ds(*cuts[h])
        return send(pre_src.at[g, :, cols], pre_land.at[g, :, cols], s_p.at[h, g], r_p.at[h, g], other)

    loads[9].wait()
    theirs = tokens_of(1 - c)
    for h, (low, count) in enumerate(cuts):
        for g in range(4):
            pre_src[g, :, low : low + count] = decoded(theirs, g, h).astype(BF16)
            to_other(h, g).start()
    ours = tokens_of(c)

    def e1(h, t):
        to_x, to_y = lax.rem(x + around(t // 4, 4), 4), lax.rem(y + around(lax.rem(t, 4), 4), 4)
        rows = pl.ds(pl.multiple_of(32 * lax.rem(to_y, 2) + 16 * (to_y // 2), 16), 16)
        cols = pl.ds(*cuts[h])
        return send(
            e_src.at[t // 4, rows, cols], land_e1.at[t, :, cols], s_e1.at[h, t], r_e1.at[h, t], plane_at(to_x, to_y)
        )

    for h, (low, count) in enumerate(cuts):
        for g in range(4):
            own = decoded(ours, g, h)
            to_other(h, g).wait_recv()
            own += pre_land[g, :, low : low + count].astype(F32)
            if g == 3:
                e_own[:, low : low + count] = own
            e_src[g, :, low : low + count] = own.astype(BF16)

            @pl.loop(4 * g, min(4 * g + 4, 15))
            def _(t, h=h):
                e1(h, t).start()

    def layer(h, stream):
        squares = jnp.zeros((32, 128), F32)
        for j in range(T):
            tile = stream[:, 128 * j : 128 * j + 128]
            squares += tile * tile
        scale = lax.rsqrt(jnp.sum(squares, axis=1, keepdims=True) / D + EPS)
        for g in range(7):
            cols = slice(512 * g, 512 * g + 512)
            lhs_f[h, :, cols] = (stream[:, cols] * scale * gpre_row[0:1, cols]).astype(BF16)
        gate_out = lax.dot_general(lhs_f[h], gate[...], (((1,), (1,)), ((), ())), preferred_element_type=F32)
        up_out = lax.dot_general(lhs_f[h], up[...], (((1,), (1,)), ((), ())), preferred_element_type=F32)
        act = (gelu(gate_out) * up_out).astype(BF16)
        for g in range(4):
            part = jnp.dot(act, d2[:, 896 * g : 896 * g + 896], preferred_element_type=F32)
            for half in range(2):
                piece = part[:, 448 * half : 448 * half + 448]
                f_own[h, 2 * g + half, :, 0:448] = piece
                f_src[h, 2 * g + half, :, 0:448] = piece.astype(BF16)

    for q in range(8):
        clean = clean_all[r * 8 + q].astype(F32)
        for j in range(T):
            clean_u[4 * q : 4 * q + 4, 128 * j : 128 * j + 128] = clean[4 * j : 4 * j + 4, :]
    loads[10].wait()
    loads[11].wait()
    loads[12].wait()
    layer(0, clean_u)

    row = pl.multiple_of(32 * yl + 16 * yh, 16)

    def e2(h, t):
        cols = pl.ds(*cuts[h])
        return send(send_e2.at[:, cols], land_e2.at[t, :, cols], s_e2.at[h, t], r_e2.at[h, t], in_z(t))

    def e3(h, t, at):
        cols = pl.ds(*cuts[h])
        return send(recon_p.at[at, :, cols], recon_p.at[at, :, cols], s_e3.at[h, t], r_e3.at[h, t], in_k(t))

    def f1(h, q, t):
        rows = pl.ds(16 * q, 16)
        return send(
            f_src.at[h, k_at(t), rows, :], land_f1.at[h, t, rows, :], s_f1.at[h, q, t], r_f1.at[h, q, t], in_k(t)
        )

    def f2(h, q, t):
        rows = pl.ds(16 * q, 16)
        return send(
            send_f2.at[h, rows, :], land_f2.at[h, t, rows, :], s_f2.at[h, q, t], r_f2.at[h, q, t], in_z(t)
        )

    def f3(h, t):
        return send(send_f3.at[h], land_f3.at[h, t], s_f3.at[h, t], r_f3.at[h, t], in_k(t))

    def start_f1(h):
        for q in range(2):

            @pl.loop(0, 7)
            def _(t, q=q):
                f1(h, q, t).start()

    sums = []
    for h, (low, count) in enumerate(cuts):
        for t in range(15):
            e1(h, t).wait_recv()
        total = e_own[pl.ds(row, 16), low : low + count]
        for t in range(15):
            total += land_e1[t, :, low : low + count].astype(F32)
        send_e2[:, low : low + count] = total.astype(BF16)

        @pl.loop(0, 7)
        def _(t, h=h):
            e2(h, t).start()

        sums.append(total)

    start_f1(0)

    for h, (low, count) in enumerate(cuts):
        for t in range(7):
            e2(h, t).wait_recv()
        for t in range(7):
            sums[h] += land_e2[t, :, low : low + count].astype(F32)
        recon_p[k, :, low : low + count] = (sums[h] + db_row[x, 0:1, low : low + count]).astype(BF16)

        @pl.loop(0, 7)
        def _(t, h=h):
            e3(h, t, k).start()

    def sum_over_k(h):
        for q in range(2):
            rows = slice(16 * q, 16 * q + 16)
            for t in range(7):
                f1(h, q, t).wait_recv()
            total = f_own[h, k, rows, :]
            for t in range(7):
                total += land_f1[h, t, rows, :].astype(F32)
            f_sum[h, rows, :] = total
            send_f2[h, rows, :] = total.astype(BF16)

            @pl.loop(0, 7)
            def _(t, q=q):
                f2(h, q, t).start()

    diagonal = (
        lax.broadcasted_iota(jnp.int32, (32, 128), 0) == lax.broadcasted_iota(jnp.int32, (32, 128), 1)
    ).astype(F32)

    def sum_over_z(h):
        for q in range(2):
            for t in range(7):
                f2(h, q, t).wait_recv()
        total = f_sum[h]
        for t in range(7):
            total += land_f2[h, t].astype(F32)
        second[h, :, 0:512] = total
        squares = jnp.sum(total * total, axis=1, keepdims=True)
        flat = jnp.sum(squares * diagonal, axis=0, keepdims=True)
        send_f3[h] = jnp.broadcast_to(flat, (8, 128))

        @pl.loop(0, 7)
        def _(t):
            f3(h, t).start()

    def outputs(h, stream):
        for t in range(7):
            f3(h, t).wait_recv()
        flat = send_f3[h]
        for t in range(7):
            flat += land_f3[h, t]
        squares = jnp.sum(flat[0:1, :] * diagonal, axis=1, keepdims=True)
        gain = pick(gpost_row, 56 * s, 8)[0:1, :]
        return pick(stream, 56 * s, 32) + pick(second.at[h], 56 * z, 32) * lax.rsqrt(squares / D + EPS) * gain

    sum_over_k(0)

    for h in range(2):
        for t in range(7):
            e3(h, t, k_from(t)).wait_recv()
    for q in range(8):
        row, col = 16 * (q % 2), 896 * (q // 2)
        recon_u[row : row + 16, col : col + 896] = recon_p[q].astype(F32)
    layer(1, recon_u)

    start_f1(1)

    sum_over_z(0)
    sum_over_k(1)
    clean_out = outputs(0, clean_u)
    sum_over_z(1)
    delta_o[...] = outputs(1, recon_u) - clean_out

    @pl.loop(0, 7)
    def _(t):
        for h in range(2):
            b1(h, t).wait_send()
            b2(h, t).wait_send()
            e2(h, t).wait_send()
            e3(h, t, k).wait_send()
            f3(h, t).wait_send()
            for q in range(2):
                f1(h, q, t).wait_send()
                f2(h, q, t).wait_send()

    @pl.loop(0, 15)
    def _(t):
        spread(t).wait_send()
        for h in range(2):
            e1(h, t).wait_send()

    @pl.loop(0, 16)
    def _(t):
        forward(t, mine).wait_send()

    for h in range(2):
        for g in range(4):
            to_other(h, g).wait_send()


def on_device(
    hidden_in, resid, down_one, gain_one, enc_weight, enc_bias, dec_weight, dec_bias, gain_pre, gate_two, up_two,
    down_two, gain_post,
):
    tiles = (T, 128)
    args = (
        hidden_in, resid, down_one, gain_one.reshape(tiles), enc_weight, enc_bias.reshape(1, 256), dec_weight,
        dec_bias.reshape(tiles), gain_pre.reshape(tiles), gate_two.T, up_two.T, down_two,
        gain_post.reshape(tiles),
    )
    dma = pltpu.SemaphoreType.DMA
    vmem = pltpu.VMEM
    latents, delta = pl.pallas_call(
        kernel,
        name="spliced",
        out_shape=(vmem((128, 256), BF16), vmem((32, 128), F32)),
        in_specs=[pl.BlockSpec(memory_space=pl.ANY)] * len(args),
        out_specs=[pl.BlockSpec(memory_space=pltpu.VMEM)] * 2,
        scratch_shapes=[vmem(a.shape, a.dtype) for a in args]
        + [
            vmem((8, 112, 128), F32),
            vmem((8, 112, 128), BF16),
            vmem((8, 112, 128), BF16),
            vmem((112, 128), BF16),
            vmem((8, 112, 128), BF16),
            vmem((8, 112, 128), F32),
            vmem((112, 128), F32),
            vmem((112, 128), F32),
            vmem((4, 8, 896), F32),
            vmem((8, D), F32),
            vmem((8, D + 128), F32),
            vmem((32, 112, 128), BF16),
            vmem((4, 32, D), F32),
            vmem((128, D), BF16),
            vmem((128, 256), BF16),
            vmem((4, 64, 896), BF16),
            vmem((4, 64, 896), BF16),
            vmem((4, 64, 896), BF16),
            vmem((64, 896), F32),
            vmem((16, 16, 896), BF16),
            vmem((16, 896), BF16),
            vmem((8, 16, 896), BF16),
            vmem((8, 16, 896), BF16),
            vmem((32, D + 128), F32),
            vmem((32, D + 128), F32),
            vmem((2, 32, D), BF16),
            vmem((2, 8, 32, 512), BF16),
            vmem((2, 8, 32, 512), F32),
            vmem((2, 8, 32, 512), BF16),
            vmem((2, 32, 512), F32),
            vmem((2, 32, 512), BF16),
            vmem((2, 8, 32, 512), BF16),
            vmem((2, 32, 640), F32),
            vmem((2, 8, 128), F32),
            vmem((2, 8, 8, 128), F32),
            dma((13,)),
            dma((2, 7)), dma((2, 7)), dma((2, 7)), dma((2, 7)),
            dma((15,)), dma((15,)), dma((16,)), dma((16,)),
            dma((2, 4)), dma((2, 4)), dma((2, 15)), dma((2, 15)),
            dma((2, 7)), dma((2, 7)), dma((2, 7)), dma((2, 7)),
            dma((2, 2, 7)), dma((2, 2, 7)), dma((2, 2, 7)), dma((2, 2, 7)), dma((2, 7)), dma((2, 7)),
        ],
        compiler_params=pltpu.CompilerParams(
            collective_id=0, has_side_effects=True, vmem_limit_bytes=62 * 2**20
        ),
        cost_estimate=pl.CostEstimate(flops=10**9, bytes_accessed=12 * 10**6, transcendentals=10**5),
    )(*args)
    return latents, delta[:, :56]


def solution(mesh):
    in_specs = (
        P("rows", "shard"),
        P("rows", None),
        P("shard", None),
        P(),
        P(None, ("rows", "shard")),
        P(("rows", "shard")),
        P(("rows", "shard"), None),
        P(),
        P(),
        P(None, "shard"),
        P(None, "shard"),
        P("shard", None),
        P(),
    )
    out_specs = (P(None, ("rows", "shard")), P("rows", "shard"))
    return jax.shard_map(on_device, mesh=mesh, in_specs=in_specs, out_specs=out_specs, check_vma=False)
```

time: 80 us -> 75.2 us (0.940)
  Pallas kernels: 77.9 us -> 73.2 us
    pallas_call x1, Pallas kernels: 77.9 us -> 73.2 us  [on_device(): pl.pallas_call(kernel, name='spliced', out_shape=(vmem((128, 256), BF16),...]
where the time goes in v3:
time: 75.2 us; the launch traced here: 75.1 us
  Pallas kernels  73.2 us (97%)
  local copies, waits for them, and re-layouts  1.24 us (2%)
    pallas_call x1, Pallas kernels, on_device(): pl.pallas_call(kernel, name='spliced', out_shape=(vmem((128, 256), BF16),...  73.2 us

profile of v3, /device:TPU:8, one launch (start us, length us, event | category | flops | bytes accessed | tf_op | source)
XLA Modules:
  0.0 75.1 jit_solution(5344572490992484635)
XLA Ops:
  0.6 73.2 %spliced.1 = (bf16[128,256]{1,0:T(8,128)(2,1)S(1)}, f32[32,128]{1,0:T(8,128)S(1)}) custom-call(bf16[32,224]{1,0:T(8,128)(2,1)} %hid_h.1, bf16[32,3584]{1,0:T(8,128)(2,1)} %resid_h.1, bf16[224,3584]{1,0:T(8,128)(2,1)} %d1_h.1, f32[28,128]{1,0:T(8,128)} %bitcast.11, bf16[3584,256]{1,0:T(8,128)(2,1)} %enc_h.1, f32[1,256]{1,0:T(1,128)} %bitcast.15, ...), custom_call_target="tpu_custom_call" | custom-call | flops 1000000000 | bytes 12000000 | tf_op jit(solution)/shard_map/spliced/pallas_call | solution.py:462
  73.9 0.6 copy.17
  74.5 0.6 copy.18

commit v4 on v3

--- a/solution.py
+++ b/solution.py
@@ -36,9 +36,9 @@
     lat_o, delta_o,
     hid, resid, d1, g1, enc, eb, dec, db, gpre, gate, up, d2, gpost,
     parts, parts_b, land_b1, send_b2, land_b2, resid_c, g1_c, db_c, db_row, gpre_row, gpost_row,
-    clean_all, cent, lhs, lat, pre_src, pre_land, e_src, e_own, land_e1, send_e2, land_e2, recon_p,
+    clean_all, cent, lhs, lat, lat_src, lat_land, e_src, e_own, land_e1, send_e2, land_e2, recon_p,
     clean_u, recon_u, lhs_f, f_src, f_own, land_f1, f_sum, send_f2, land_f2, second, send_f3, land_f3,
-    load_sem, s_b1, r_b1, s_b2, r_b2, s_c, r_c, s_cc, r_cc, s_p, r_p, s_e1, r_e1, s_e2, r_e2, s_e3, r_e3,
+    d1_sem, load_sem, s_b1, r_b1, s_b2, r_b2, s_w, r_w, s_c, r_c, s_l, r_l, s_e1, r_e1, s_e2, r_e2, s_e3, r_e3,
     s_f1, r_f1, s_f2, r_f2, s_f3, r_f3,
 ):
     r = lax.axis_index("rows")
@@ -46,7 +46,7 @@
     yl, c = r // 2, lax.rem(r, 2)
     k, z = s // 8, lax.rem(s, 8)
     x, yh = k // 2, lax.rem(k, 2)
-    y = 2 * yh + yl
+    y, m = 2 * yh + yl, yl * 8 + k
     other = (yl * 2 + 1 - c, s)
 
     def k_at(t):
@@ -67,27 +67,33 @@
     def in_plane(t):
         return plane_at(lax.rem(x + around(t // 4, 4), 4), lax.rem(y + around(lax.rem(t, 4), 4), 4))
 
-    def chunk_from(t, core):
+    def chunk_from(t):
         from_x = lax.rem(x + 4 - around(t // 4, 4), 4)
         from_y = lax.rem(y + 4 - around(lax.rem(t, 4), 4), 4)
-        return (lax.rem(from_y, 2) * 2 + core) * 8 + from_x * 2 + from_y // 2
+        return lax.rem(from_y, 2) * 8 + from_x * 2 + from_y // 2
 
     def send(src, dst, s_sem, r_sem, device):
         return pltpu.make_async_remote_copy(
             src_ref=src, dst_ref=dst, send_sem=s_sem, recv_sem=r_sem, device_id=device, device_id_type=MESH
         )
+
+    def first_load(g):
+        cols = pl.ds(512 * g, 512)
+        return pltpu.make_async_copy(d1_h.at[:, cols], d1.at[:, cols], d1_sem.at[g])
 
     loads = [
         pltpu.make_async_copy(a, b, load_sem.at[i])
         for i, (a, b) in enumerate(
             (
-                (hid_h, hid), (d1_h, d1), (resid_h, resid), (g1_h, g1), (db_h, db), (gpre_h, gpre), (gpost_h, gpost),
-                (eb_h, eb), (enc_h, enc), (dec_h, dec), (gate_h, gate), (up_h, up), (d2_h, d2),
+                (hid_h, hid), (resid_h, resid), (g1_h, g1), (db_h, db), (gpre_h, gpre), (gpost_h, gpost),
+                (eb_h, eb.at[:, pl.ds(0, 256)]), (enc_h, enc.at[:, pl.ds(0, 256)]), (dec_h, dec.at[pl.ds(0, 256), :]),
+                (gate_h, gate), (up_h, up), (d2_h, d2),
             )
         )
     ]
-    for load in loads:
-        load.start()
+    loads[0].start()
+    for g in range(7):
+        first_load(g).start()
 
     barrier = pltpu.get_barrier_semaphore()
 
@@ -101,34 +107,50 @@
 
     pl.semaphore_signal(barrier, inc=1, device_id=other, device_id_type=MESH)
 
+    thirds = ((0, 32), (32, 32), (64, 48))
+
+    def b1(h, t):
+        rows = pl.ds(*thirds[h])
+        return send(
+            parts_b.at[k_at(t), rows, :], land_b1.at[t, rows, :], s_b1.at[h, t], r_b1.at[h, t], in_k(t)
+        )
+
     loads[0].wait()
-    loads[1].wait()
     for g in range(7):
+        first_load(g).wait()
         part = jnp.dot(hid[...], d1[:, 512 * g : 512 * g + 512], preferred_element_type=F32)
         for j in range(4):
             row = 4 * (4 * g + j)
             for piece in range(8):
                 parts[piece, row : row + 4, :] = part[4 * piece : 4 * piece + 4, 128 * j : 128 * j + 128]
-    for piece in range(8):
-        parts_b[piece] = parts[piece].astype(BF16)
-
-    pl.semaphore_wait(barrier, 23)
-
-    halves = ((0, 64), (64, 48))
-
-    def b1(h, t):
-        rows = pl.ds(*halves[h])
-        return send(
-            parts_b.at[k_at(t), rows, :], land_b1.at[t, rows, :], s_b1.at[h, t], r_b1.at[h, t], in_k(t)
-        )
-
-    for h in range(2):
-
-        @pl.loop(0, 7)
-        def _(t, h=h):
-            b1(h, t).start()
-
-    for i in range(2, 8):
+        if g in (1, 3, 6):
+            h = (1, 3, 6).index(g)
+            rows = slice(thirds[h][0], sum(thirds[h]))
+            for piece in range(8):
+                parts_b[piece, rows, :] = parts[piece, rows, :].astype(BF16)
+            if h == 0:
+                pl.semaphore_wait(barrier, 23)
+
+            @pl.loop(0, 7)
+            def _(t, h=h):
+                b1(h, t).start()
+
+    for load in loads[1:]:
+        load.start()
+    shared = [
+        send(a, b, s_w.at[i], r_w.at[i], other)
+        for i, (a, b) in enumerate(
+            (
+                (eb_h, eb.at[:, pl.ds(256, 256)]),
+                (enc_h, enc.at[:, pl.ds(256, 256)]),
+                (dec_h, dec.at[pl.ds(256, 256), :]),
+            )
+        )
+    ]
+    for share in shared:
+        share.start()
+
+    for i in range(1, 7):
         loads[i].wait()
     for j in range(T):
         tile = slice(128 * j, 128 * j + 128)
@@ -148,11 +170,11 @@
     f_own[:, :, :, 448:] = jnp.zeros((2, 8, 32, 64), F32)
 
     def b2(h, t):
-        rows = pl.ds(*halves[h])
+        rows = pl.ds(*thirds[h])
         return send(send_b2.at[rows, :], land_b2.at[t, rows, :], s_b2.at[h, t], r_b2.at[h, t], in_z(t))
 
     sums = []
-    for h, (low, count) in enumerate(halves):
+    for h, (low, count) in enumerate(thirds):
         for t in range(7):
             b1(h, t).wait_recv()
         total = parts[k, low : low + count, :]
@@ -166,7 +188,7 @@
 
         sums.append(total)
 
-    for h, (low, count) in enumerate(halves):
+    for h, (low, count) in enumerate(thirds):
         for t in range(7):
             b2(h, t).wait_recv()
         for t in range(7):
@@ -178,75 +200,36 @@
     squares += pltpu.roll(squares, 4, 0)
     scale = lax.rsqrt(jnp.sum(squares, axis=1, keepdims=True) / D + EPS)
     scale = jnp.concatenate([jnp.broadcast_to(scale, (8, 128))] * 14, axis=0)
-    mine = r * 8 + k
-    clean_all[mine] = (resid_c[k] + total * scale * g1_c[...]).astype(BF16)
+    clean_all[m] = (resid_c[k] + total * scale * g1_c[...]).astype(BF16)
 
     def spread(t):
-        return send(clean_all.at[mine], clean_all.at[mine], s_c.at[t], r_c.at[t], in_plane(t))
-
-    def forward(t, at):
-        return send(clean_all.at[at], clean_all.at[at], s_cc.at[t], r_cc.at[t], other)
-
-    def place(core):
-        @pl.loop(0, 2)
-        def _(low):
-            group = low * 2 + core
-            for q in range(8):
-                centered = (clean_all[group * 8 + q].astype(F32) - db_c[...]).astype(BF16).astype(F32)
-                for j in range(T):
-                    cent[group, 4 * q : 4 * q + 4, 128 * j : 128 * j + 128] = centered[4 * j : 4 * j + 4, :]
-            lhs[pl.ds(pl.multiple_of(group * 32, 32), 32), :] = cent[group].astype(BF16)
+        return send(clean_all.at[m], clean_all.at[m], s_c.at[t], r_c.at[t], in_plane(t))
 
     @pl.loop(0, 15)
     def _(t):
         spread(t).start()
 
-    forward(15, mine).start()
-
     @pl.loop(0, 15)
-    def _(i):
-        t = 14 - i
-        at = chunk_from(t, c)
+    def _(t):
+        at = chunk_from(t)
         send(clean_all.at[at], clean_all.at[at], s_c.at[t], r_c.at[t], in_plane(t)).wait_recv()
-        forward(t, at).start()
-
-    place(c)
-
-    @pl.loop(0, 16)
-    def _(i):
-        t = 15 - i
-        at = chunk_from(t, 1 - c)
-        forward(t, at).wait_recv()
-
-    place(1 - c)
-    loads[8].wait()
+
+    for low in range(2):
+        for q in range(8):
+            centered = (clean_all[low * 8 + q].astype(F32) - db_c[...]).astype(BF16).astype(F32)
+            for j in range(T):
+                cent[low, 4 * q : 4 * q + 4, 128 * j : 128 * j + 128] = centered[4 * j : 4 * j + 4, :]
+        lhs[32 * low : 32 * low + 32, :] = cent[low].astype(BF16)
+
+    loads[7].wait()
+    for share in shared:
+        share.wait_recv()
     pre_act = jnp.dot(lhs[...], enc[...], preferred_element_type=F32) + eb[...]
     lat[...] = jnp.maximum(pre_act, 0.0).astype(BF16)
-    lat_o[...] = lat[...]
-
-    cuts = ((0, 512), (512, 384))
-
-    def tokens_of(core):
-        low = lat[pl.ds(pl.multiple_of(core * 32, 32), 32), :]
-        high = lat[pl.ds(pl.multiple_of(core * 32 + 64, 32), 32), :]
-        return jnp.concatenate([low, high], axis=0)
-
-    def decoded(tokens, g, h):
-        first_col = lax.rem(x + around(jnp.int32(g), 4), 4) * 896 + cuts[h][0]
-        cols = pl.ds(pl.multiple_of(first_col, 128), cuts[h][1])
-        return jnp.dot(tokens, dec[:, cols], preferred_element_type=F32)
-
-    def to_other(h, g):
-        cols = pl.ds(*cuts[h])
-        return send(pre_src.at[g, :, cols], pre_land.at[g, :, cols], s_p.at[h, g], r_p.at[h, g], other)
-
-    loads[9].wait()
-    theirs = tokens_of(1 - c)
-    for h, (low, count) in enumerate(cuts):
-        for g in range(4):
-            pre_src[g, :, low : low + count] = decoded(theirs, g, h).astype(BF16)
-            to_other(h, g).start()
-    ours = tokens_of(c)
+    lat_src[...] = lat[:, 256:512]
+    swap = send(lat_src, lat_land, s_l.at[0], r_l.at[0], other)
+
+    cuts = ((0, 384), (384, 256), (640, 256))
 
     def e1(h, t):
         to_x, to_y = lax.rem(x + around(t // 4, 4), 4), lax.rem(y + around(lax.rem(t, 4), 4), 4)
@@ -256,11 +239,12 @@
             e_src.at[t // 4, rows, cols], land_e1.at[t, :, cols], s_e1.at[h, t], r_e1.at[h, t], plane_at(to_x, to_y)
         )
 
+    loads[8].wait()
     for h, (low, count) in enumerate(cuts):
         for g in range(4):
-            own = decoded(ours, g, h)
-            to_other(h, g).wait_recv()
-            own += pre_land[g, :, low : low + count].astype(F32)
+            first_col = lax.rem(x + around(jnp.int32(g), 4), 4) * 896 + low
+            cols = pl.ds(pl.multiple_of(first_col, 128), count)
+            own = jnp.dot(lat[...], dec[:, cols], preferred_element_type=F32)
             if g == 3:
                 e_own[:, low : low + count] = own
             e_src[g, :, low : low + count] = own.astype(BF16)
@@ -268,6 +252,8 @@
             @pl.loop(4 * g, min(4 * g + 4, 15))
             def _(t, h=h):
                 e1(h, t).start()
+
+    swap.start()
 
     def layer(h, stream):
         squares = jnp.zeros((32, 128), F32)
@@ -289,12 +275,12 @@
                 f_src[h, 2 * g + half, :, 0:448] = piece.astype(BF16)
 
     for q in range(8):
-        clean = clean_all[r * 8 + q].astype(F32)
+        clean = clean_all[yl * 8 + q].astype(F32)
         for j in range(T):
             clean_u[4 * q : 4 * q + 4, 128 * j : 128 * j + 128] = clean[4 * j : 4 * j + 4, :]
+    loads[9].wait()
     loads[10].wait()
     loads[11].wait()
-    loads[12].wait()
     layer(0, clean_u)
 
     row = pl.multiple_of(32 * yl + 16 * yh, 16)
@@ -404,7 +390,7 @@
 
     sum_over_k(0)
 
-    for h in range(2):
+    for h in range(3):
         for t in range(7):
             e3(h, t, k_from(t)).wait_recv()
     for q in range(8):
@@ -420,13 +406,20 @@
     sum_over_z(1)
     delta_o[...] = outputs(1, recon_u) - clean_out
 
+    swap.wait_recv()
+    for low in range(2):
+        rows = slice(32 * low, 32 * low + 32)
+        lat_o[pl.ds(pl.multiple_of(64 * low + 32 * c, 32), 32), :] = lat[rows, 0:256]
+        lat_o[pl.ds(pl.multiple_of(64 * low + 32 - 32 * c, 32), 32), :] = lat_land[rows, :]
+
     @pl.loop(0, 7)
     def _(t):
-        for h in range(2):
+        for h in range(3):
             b1(h, t).wait_send()
             b2(h, t).wait_send()
             e2(h, t).wait_send()
             e3(h, t, k).wait_send()
+        for h in range(2):
             f3(h, t).wait_send()
             for q in range(2):
                 f1(h, q, t).wait_send()
@@ -435,16 +428,12 @@
     @pl.loop(0, 15)
     def _(t):
         spread(t).wait_send()
-        for h in range(2):
+        for h in range(3):
             e1(h, t).wait_send()
 
-    @pl.loop(0, 16)
-    def _(t):
-        forward(t, mine).wait_send()
-
-    for h in range(2):
-        for g in range(4):
-            to_other(h, g).wait_send()
+    swap.wait_send()
+    for share in shared:
+        share.wait_send()
 
 
 def on_device(
@@ -457,6 +446,7 @@
         dec_bias.reshape(tiles), gain_pre.reshape(tiles), gate_two.T, up_two.T, down_two,
         gain_post.reshape(tiles),
     )
+    held = {4: (D, 512), 5: (1, 512), 6: (512, D)}
     dma = pltpu.SemaphoreType.DMA
     vmem = pltpu.VMEM
     latents, delta = pl.pallas_call(
@@ -465,7 +455,7 @@
         out_shape=(vmem((128, 256), BF16), vmem((32, 128), F32)),
         in_specs=[pl.BlockSpec(memory_space=pl.ANY)] * len(args),
         out_specs=[pl.BlockSpec(memory_space=pltpu.VMEM)] * 2,
-        scratch_shapes=[vmem(a.shape, a.dtype) for a in args]
+        scratch_shapes=[vmem(held.get(i, a.shape), a.dtype) for i, a in enumerate(args)]
         + [
             vmem((8, 112, 128), F32),
             vmem((8, 112, 128), BF16),
@@ -478,12 +468,12 @@
             vmem((4, 8, 896), F32),
             vmem((8, D), F32),
             vmem((8, D + 128), F32),
-            vmem((32, 112, 128), BF16),
-            vmem((4, 32, D), F32),
-            vmem((128, D), BF16),
-            vmem((128, 256), BF16),
-            vmem((4, 64, 896), BF16),
-            vmem((4, 64, 896), BF16),
+            vmem((16, 112, 128), BF16),
+            vmem((2, 32, D), F32),
+            vmem((64, D), BF16),
+            vmem((64, 512), BF16),
+            vmem((64, 256), BF16),
+            vmem((64, 256), BF16),
             vmem((4, 64, 896), BF16),
             vmem((64, 896), F32),
             vmem((16, 16, 896), BF16),
@@ -502,11 +492,10 @@
             vmem((2, 32, 640), F32),
             vmem((2, 8, 128), F32),
             vmem((2, 8, 8, 128), F32),
-            dma((13,)),
-            dma((2, 7)), dma((2, 7)), dma((2, 7)), dma((2, 7)),
-            dma((15,)), dma((15,)), dma((16,)), dma((16,)),
-            dma((2, 4)), dma((2, 4)), dma((2, 15)), dma((2, 15)),
-            dma((2, 7)), dma((2, 7)), dma((2, 7)), dma((2, 7)),
+            dma((7,)), dma((12,)),
+            dma((3, 7)), dma((3, 7)), dma((3, 7)), dma((3, 7)),
+            dma((3,)), dma((3,)), dma((15,)), dma((15,)), dma((1,)), dma((1,)),
+            dma((3, 15)), dma((3, 15)), dma((3, 7)), dma((3, 7)), dma((3, 7)), dma((3, 7)),
             dma((2, 2, 7)), dma((2, 2, 7)), dma((2, 2, 7)), dma((2, 2, 7)), dma((2, 7)), dma((2, 7)),
         ],
         compiler_params=pltpu.CompilerParams(

time: 75.2 us -> 71.4 us (0.949); the launches traced: 75.1 us -> 70.4 us
  Pallas kernels: 73.2 us -> 68.5 us
    pallas_call x1, Pallas kernels: 73.2 us -> 68.5 us  [on_device(): pl.pallas_call(kernel, name='spliced', out_shape=(vmem((128, 256), BF16),...]
where the time goes in v4:
time: 71.4 us; the launch traced here: 70.4 us
  Pallas kernels  68.5 us (96%)
  local copies, waits for them, and re-layouts  1.24 us (2%)
    pallas_call x1, Pallas kernels, on_device(): pl.pallas_call(kernel, name='spliced', out_shape=(vmem((128, 256), BF16),...  68.5 us

profile of v4, /device:TPU:8, one launch (start us, length us, event | category | flops | bytes accessed | tf_op | source)
XLA Modules:
  0.0 70.4 jit_solution(733846013016072887)
XLA Ops:
  0.6 68.5 %spliced.1 = (bf16[128,256]{1,0:T(8,128)(2,1)S(1)}, f32[32,128]{1,0:T(8,128)S(1)}) custom-call(bf16[32,224]{1,0:T(8,128)(2,1)} %hid_h.1, bf16[32,3584]{1,0:T(8,128)(2,1)} %resid_h.1, bf16[224,3584]{1,0:T(8,128)(2,1)} %d1_h.1, f32[28,128]{1,0:T(8,128)} %bitcast.11, bf16[3584,256]{1,0:T(8,128)(2,1)} %enc_h.1, f32[1,256]{1,0:T(1,128)} %bitcast.15, ...), custom_call_target="tpu_custom_call" | custom-call | flops 1000000000 | bytes 12000000 | tf_op jit(solution)/shard_map/spliced/pallas_call | solution.py:452
  69.1 0.6 copy.17
  69.8 0.6 copy.18

commit v5 on v4

--- a/solution.py
+++ b/solution.py
@@ -24,7 +24,7 @@
 
 
 def around(t, n):
-    return lax.rem(n // 2 + n + (1 - 2 * lax.rem(t, 2)) * ((t + 1) // 2), n)
+    return (n // 2 + n + (1 - 2 * (t % 2)) * ((t + 1) // 2)) % n
 
 
 def gelu(v):
@@ -50,10 +50,10 @@
     other = (yl * 2 + 1 - c, s)
 
     def k_at(t):
-        return lax.rem(x + around(t // 2, 4), 4) * 2 + lax.rem(yh + 1 - lax.rem(t, 2), 2)
+        return lax.rem(x + around(t // 2, 4), 4) * 2 + lax.rem(yh + 1 - t % 2, 2)
 
     def k_from(t):
-        return lax.rem(x + 4 - around(t // 2, 4), 4) * 2 + lax.rem(yh + 1 - lax.rem(t, 2), 2)
+        return lax.rem(x + 4 - around(t // 2, 4), 4) * 2 + lax.rem(yh + 1 - t % 2, 2)
 
     def in_k(t):
         return (r, k_at(t) * 8 + z)
@@ -65,11 +65,11 @@
         return (lax.rem(to_y, 2) * 2 + c, (to_x * 2 + to_y // 2) * 8 + z)
 
     def in_plane(t):
-        return plane_at(lax.rem(x + around(t // 4, 4), 4), lax.rem(y + around(lax.rem(t, 4), 4), 4))
+        return plane_at(lax.rem(x + around(t // 4, 4), 4), lax.rem(y + around(t % 4, 4), 4))
 
     def chunk_from(t):
         from_x = lax.rem(x + 4 - around(t // 4, 4), 4)
-        from_y = lax.rem(y + 4 - around(lax.rem(t, 4), 4), 4)
+        from_y = lax.rem(y + 4 - around(t % 4, 4), 4)
         return lax.rem(from_y, 2) * 8 + from_x * 2 + from_y // 2
 
     def send(src, dst, s_sem, r_sem, device):
@@ -96,13 +96,9 @@
         first_load(g).start()
 
     barrier = pltpu.get_barrier_semaphore()
-
-    @pl.loop(0, 15)
-    def _(t):
+    for t in range(15):
         pl.semaphore_signal(barrier, inc=1, device_id=in_plane(t), device_id_type=MESH)
-
-    @pl.loop(0, 7)
-    def _(t):
+    for t in range(7):
         pl.semaphore_signal(barrier, inc=1, device_id=in_z(t), device_id_type=MESH)
 
     pl.semaphore_signal(barrier, inc=1, device_id=other, device_id_type=MESH)
@@ -130,9 +126,7 @@
                 parts_b[piece, rows, :] = parts[piece, rows, :].astype(BF16)
             if h == 0:
                 pl.semaphore_wait(barrier, 23)
-
-            @pl.loop(0, 7)
-            def _(t, h=h):
+            for t in range(7):
                 b1(h, t).start()
 
     for load in loads[1:]:
@@ -166,8 +160,6 @@
     clean_u[:, D:] = jnp.zeros((32, 128), F32)
     recon_u[:, D:] = jnp.zeros((32, 128), F32)
     second[:, :, 448:] = jnp.zeros((2, 32, 192), F32)
-    f_src[:, :, :, 448:] = jnp.zeros((2, 8, 32, 64), BF16)
-    f_own[:, :, :, 448:] = jnp.zeros((2, 8, 32, 64), F32)
 
     def b2(h, t):
         rows = pl.ds(*thirds[h])
@@ -181,9 +173,7 @@
         for t in range(7):
             total += land_b1[t, low : low + count, :].astype(F32)
         send_b2[low : low + count, :] = total.astype(BF16)
-
-        @pl.loop(0, 7)
-        def _(t, h=h):
+        for t in range(7):
             b2(h, t).start()
 
         sums.append(total)
@@ -205,12 +195,10 @@
     def spread(t):
         return send(clean_all.at[m], clean_all.at[m], s_c.at[t], r_c.at[t], in_plane(t))
 
-    @pl.loop(0, 15)
-    def _(t):
+    for t in range(15):
         spread(t).start()
 
-    @pl.loop(0, 15)
-    def _(t):
+    for t in range(15):
         at = chunk_from(t)
         send(clean_all.at[at], clean_all.at[at], s_c.at[t], r_c.at[t], in_plane(t)).wait_recv()
 
@@ -232,7 +220,7 @@
     cuts = ((0, 384), (384, 256), (640, 256))
 
     def e1(h, t):
-        to_x, to_y = lax.rem(x + around(t // 4, 4), 4), lax.rem(y + around(lax.rem(t, 4), 4), 4)
+        to_x, to_y = lax.rem(x + around(t // 4, 4), 4), lax.rem(y + around(t % 4, 4), 4)
         rows = pl.ds(pl.multiple_of(32 * lax.rem(to_y, 2) + 16 * (to_y // 2), 16), 16)
         cols = pl.ds(*cuts[h])
         return send(
@@ -242,15 +230,13 @@
     loads[8].wait()
     for h, (low, count) in enumerate(cuts):
         for g in range(4):
-            first_col = lax.rem(x + around(jnp.int32(g), 4), 4) * 896 + low
+            first_col = lax.rem(x + around(g, 4), 4) * 896 + low
             cols = pl.ds(pl.multiple_of(first_col, 128), count)
             own = jnp.dot(lat[...], dec[:, cols], preferred_element_type=F32)
             if g == 3:
                 e_own[:, low : low + count] = own
             e_src[g, :, low : low + count] = own.astype(BF16)
-
-            @pl.loop(4 * g, min(4 * g + 4, 15))
-            def _(t, h=h):
+            for t in range(4 * g, min(4 * g + 4, 15)):
                 e1(h, t).start()
 
     swap.start()
@@ -271,8 +257,11 @@
             part = jnp.dot(act, d2[:, 896 * g : 896 * g + 896], preferred_element_type=F32)
             for half in range(2):
                 piece = part[:, 448 * half : 448 * half + 448]
-                f_own[h, 2 * g + half, :, 0:448] = piece
-                f_src[h, 2 * g + half, :, 0:448] = piece.astype(BF16)
+                top, low = piece[0:16, :], piece[16:32, :]
+                ends = jnp.concatenate([top[:, 384:448], low[:, 384:448]], axis=1)
+                packed = jnp.concatenate([top[:, 0:384], low[:, 0:384], ends], axis=1)
+                f_own[h, 2 * g + half] = packed
+                f_src[h, 2 * g + half] = packed.astype(BF16)
 
     for q in range(8):
         clean = clean_all[yl * 8 + q].astype(F32)
@@ -294,25 +283,23 @@
         return send(recon_p.at[at, :, cols], recon_p.at[at, :, cols], s_e3.at[h, t], r_e3.at[h, t], in_k(t))
 
     def f1(h, q, t):
-        rows = pl.ds(16 * q, 16)
+        cols = pl.ds(*cuts[q])
         return send(
-            f_src.at[h, k_at(t), rows, :], land_f1.at[h, t, rows, :], s_f1.at[h, q, t], r_f1.at[h, q, t], in_k(t)
+            f_src.at[h, k_at(t), :, cols], land_f1.at[h, t, :, cols], s_f1.at[h, q, t], r_f1.at[h, q, t], in_k(t)
         )
 
     def f2(h, q, t):
-        rows = pl.ds(16 * q, 16)
+        cols = pl.ds(*cuts[q])
         return send(
-            send_f2.at[h, rows, :], land_f2.at[h, t, rows, :], s_f2.at[h, q, t], r_f2.at[h, q, t], in_z(t)
+            send_f2.at[h, :, cols], land_f2.at[h, t, :, cols], s_f2.at[h, q, t], r_f2.at[h, q, t], in_z(t)
         )
 
     def f3(h, t):
         return send(send_f3.at[h], land_f3.at[h, t], s_f3.at[h, t], r_f3.at[h, t], in_k(t))
 
     def start_f1(h):
-        for q in range(2):
-
-            @pl.loop(0, 7)
-            def _(t, q=q):
+        for q in range(3):
+            for t in range(7):
                 f1(h, q, t).start()
 
     sums = []
@@ -323,9 +310,7 @@
         for t in range(15):
             total += land_e1[t, :, low : low + count].astype(F32)
         send_e2[:, low : low + count] = total.astype(BF16)
-
-        @pl.loop(0, 7)
-        def _(t, h=h):
+        for t in range(7):
             e2(h, t).start()
 
         sums.append(total)
@@ -338,24 +323,20 @@
         for t in range(7):
             sums[h] += land_e2[t, :, low : low + count].astype(F32)
         recon_p[k, :, low : low + count] = (sums[h] + db_row[x, 0:1, low : low + count]).astype(BF16)
-
-        @pl.loop(0, 7)
-        def _(t, h=h):
+        for t in range(7):
             e3(h, t, k).start()
 
     def sum_over_k(h):
-        for q in range(2):
-            rows = slice(16 * q, 16 * q + 16)
+        for q, (low, count) in enumerate(cuts):
+            cols = slice(low, low + count)
             for t in range(7):
                 f1(h, q, t).wait_recv()
-            total = f_own[h, k, rows, :]
-            for t in range(7):
-                total += land_f1[h, t, rows, :].astype(F32)
-            f_sum[h, rows, :] = total
-            send_f2[h, rows, :] = total.astype(BF16)
-
-            @pl.loop(0, 7)
-            def _(t, q=q):
+            total = f_own[h, k, :, cols]
+            for t in range(7):
+                total += land_f1[h, t, :, cols].astype(F32)
+            f_sum[h, :, cols] = total
+            send_f2[h, :, cols] = total.astype(BF16)
+            for t in range(7):
                 f2(h, q, t).start()
 
     diagonal = (
@@ -363,19 +344,23 @@
     ).astype(F32)
 
     def sum_over_z(h):
-        for q in range(2):
+        for q, (low, count) in enumerate(cuts):
+            cols = slice(low, low + count)
             for t in range(7):
                 f2(h, q, t).wait_recv()
-        total = f_sum[h]
-        for t in range(7):
-            total += land_f2[h, t].astype(F32)
-        second[h, :, 0:512] = total
+            total = f_sum[h, :, cols]
+            for t in range(7):
+                total += land_f2[h, t, :, cols].astype(F32)
+            f_sum[h, :, cols] = total
+        second[h, 0:16, 0:384] = f_sum[h, :, 0:384]
+        second[h, 16:32, 0:384] = f_sum[h, :, 384:768]
+        second[h, 0:16, 384:448] = f_sum[h, :, 768:832]
+        second[h, 16:32, 384:448] = f_sum[h, :, 832:896]
+        total = second[h, :, 0:512]
         squares = jnp.sum(total * total, axis=1, keepdims=True)
         flat = jnp.sum(squares * diagonal, axis=0, keepdims=True)
         send_f3[h] = jnp.broadcast_to(flat, (8, 128))
-
-        @pl.loop(0, 7)
-        def _(t):
+        for t in range(7):
             f3(h, t).start()
 
     def outputs(h, stream):
@@ -412,8 +397,7 @@
         lat_o[pl.ds(pl.multiple_of(64 * low + 32 * c, 32), 32), :] = lat[rows, 0:256]
         lat_o[pl.ds(pl.multiple_of(64 * low + 32 - 32 * c, 32), 32), :] = lat_land[rows, :]
 
-    @pl.loop(0, 7)
-    def _(t):
+    for t in range(7):
         for h in range(3):
             b1(h, t).wait_send()
             b2(h, t).wait_send()
@@ -421,12 +405,10 @@
             e3(h, t, k).wait_send()
         for h in range(2):
             f3(h, t).wait_send()
-            for q in range(2):
+            for q in range(3):
                 f1(h, q, t).wait_send()
                 f2(h, q, t).wait_send()
-
-    @pl.loop(0, 15)
-    def _(t):
+    for t in range(15):
         spread(t).wait_send()
         for h in range(3):
             e1(h, t).wait_send()
@@ -483,12 +465,12 @@
             vmem((32, D + 128), F32),
             vmem((32, D + 128), F32),
             vmem((2, 32, D), BF16),
-            vmem((2, 8, 32, 512), BF16),
-            vmem((2, 8, 32, 512), F32),
-            vmem((2, 8, 32, 512), BF16),
-            vmem((2, 32, 512), F32),
-            vmem((2, 32, 512), BF16),
-            vmem((2, 8, 32, 512), BF16),
+            vmem((2, 8, 16, 896), BF16),
+            vmem((2, 8, 16, 896), F32),
+            vmem((2, 8, 16, 896), BF16),
+            vmem((2, 16, 896), F32),
+            vmem((2, 16, 896), BF16),
+            vmem((2, 8, 16, 896), BF16),
             vmem((2, 32, 640), F32),
             vmem((2, 8, 128), F32),
             vmem((2, 8, 8, 128), F32),
@@ -496,7 +478,7 @@
             dma((3, 7)), dma((3, 7)), dma((3, 7)), dma((3, 7)),
             dma((3,)), dma((3,)), dma((15,)), dma((15,)), dma((1,)), dma((1,)),
             dma((3, 15)), dma((3, 15)), dma((3, 7)), dma((3, 7)), dma((3, 7)), dma((3, 7)),
-            dma((2, 2, 7)), dma((2, 2, 7)), dma((2, 2, 7)), dma((2, 2, 7)), dma((2, 7)), dma((2, 7)),
+            dma((2, 3, 7)), dma((2, 3, 7)), dma((2, 3, 7)), dma((2, 3, 7)), dma((2, 7)), dma((2, 7)),
         ],
         compiler_params=pltpu.CompilerParams(
             collective_id=0, has_side_effects=True, vmem_limit_bytes=62 * 2**20

time: 71.4 us -> 70.3 us (0.985); the launches traced: 70.4 us -> 70.2 us
  no operation moved by 1% of the time
where the time goes in v5:
time: 70.3 us; the launch traced here: 70.2 us
  Pallas kernels  68.3 us (97%)
  local copies, waits for them, and re-layouts  1.24 us (2%)
    pallas_call x1, Pallas kernels, on_device(): pl.pallas_call(kernel, name='spliced', out_shape=(vmem((128, 256), BF16),...  68.3 us

profile of v5, /device:TPU:8, one launch (start us, length us, event | category | flops | bytes accessed | tf_op | source)
XLA Modules:
  0.0 70.2 jit_solution(4507659447031627751)
XLA Ops:
  0.6 68.3 %spliced.1 = (bf16[128,256]{1,0:T(8,128)(2,1)S(1)}, f32[32,128]{1,0:T(8,128)S(1)}) custom-call(bf16[32,224]{1,0:T(8,128)(2,1)} %hid_h.1, bf16[32,3584]{1,0:T(8,128)(2,1)} %resid_h.1, bf16[224,3584]{1,0:T(8,128)(2,1)} %d1_h.1, f32[28,128]{1,0:T(8,128)} %bitcast.11, bf16[3584,256]{1,0:T(8,128)(2,1)} %enc_h.1, f32[1,256]{1,0:T(1,128)} %bitcast.15, ...), custom_call_target="tpu_custom_call" | custom-call | flops 1000000000 | bytes 12000000 | tf_op jit(solution)/shard_map/spliced/pallas_call | solution.py:434
  69.0 0.6 copy.17
  69.6 0.6 copy.18

commit v6 on v5

--- a/solution.py
+++ b/solution.py
@@ -389,8 +389,6 @@
     sum_over_k(1)
     clean_out = outputs(0, clean_u)
     sum_over_z(1)
-    delta_o[...] = outputs(1, recon_u) - clean_out
-
     swap.wait_recv()
     for low in range(2):
         rows = slice(32 * low, 32 * low + 32)
@@ -403,8 +401,8 @@
             b2(h, t).wait_send()
             e2(h, t).wait_send()
             e3(h, t, k).wait_send()
+        f3(0, t).wait_send()
         for h in range(2):
-            f3(h, t).wait_send()
             for q in range(3):
                 f1(h, q, t).wait_send()
                 f2(h, q, t).wait_send()
@@ -416,6 +414,10 @@
     swap.wait_send()
     for share in shared:
         share.wait_send()
+    delta_o[...] = outputs(1, recon_u) - clean_out
+
+    for t in range(7):
+        f3(1, t).wait_send()
 
 
 def on_device(

time: 70.3 us -> 69.9 us (level)
  no operation moved by 1% of the time
where the time goes in v6:
time: 69.9 us; the launch traced here: 69.8 us
  Pallas kernels  68 us (97%)
  local copies, waits for them, and re-layouts  1.24 us (2%)
    pallas_call x1, Pallas kernels, on_device(): pl.pallas_call(kernel, name='spliced', out_shape=(vmem((128, 256), BF16),...  68 us

profile of v6, /device:TPU:8, one launch (start us, length us, event | category | flops | bytes accessed | tf_op | source)
XLA Modules:
  0.0 69.8 jit_solution(12298897201048394342)
XLA Ops:
  0.6 68.0 %spliced.1 = (bf16[128,256]{1,0:T(8,128)(2,1)S(1)}, f32[32,128]{1,0:T(8,128)S(1)}) custom-call(bf16[32,224]{1,0:T(8,128)(2,1)} %hid_h.1, bf16[32,3584]{1,0:T(8,128)(2,1)} %resid_h.1, bf16[224,3584]{1,0:T(8,128)(2,1)} %d1_h.1, f32[28,128]{1,0:T(8,128)} %bitcast.11, bf16[3584,256]{1,0:T(8,128)(2,1)} %enc_h.1, f32[1,256]{1,0:T(1,128)} %bitcast.15, ...), custom_call_target="tpu_custom_call" | custom-call | flops 1000000000 | bytes 12000000 | tf_op jit(solution)/shard_map/spliced/pallas_call | solution.py:436
  68.6 0.6 copy.17
  69.2 0.6 copy.18

commit v7 on v6

--- a/solution.py
+++ b/solution.py
@@ -373,7 +373,6 @@
         gain = pick(gpost_row, 56 * s, 8)[0:1, :]
         return pick(stream, 56 * s, 32) + pick(second.at[h], 56 * z, 32) * lax.rsqrt(squares / D + EPS) * gain
 
-    sum_over_k(0)
 
     for h in range(3):
         for t in range(7):
@@ -384,11 +383,12 @@
     layer(1, recon_u)
 
     start_f1(1)
-
+    sum_over_k(0)
+
+    sum_over_k(1)
     sum_over_z(0)
-    sum_over_k(1)
+    sum_over_z(1)
     clean_out = outputs(0, clean_u)
-    sum_over_z(1)
     swap.wait_recv()
     for low in range(2):
         rows = slice(32 * low, 32 * low + 32)

time: 69.9 us -> 69 us (0.987)
  Pallas kernels: 68 us -> 66.5 us
    pallas_call x1, Pallas kernels: 68 us -> 66.5 us  [on_device(): pl.pallas_call(kernel, name='spliced', out_shape=(vmem((128, 256), BF16),...]
where the time goes in v7:
time: 69 us; the launch traced here: 68.3 us
  Pallas kernels  66.5 us (96%)
  local copies, waits for them, and re-layouts  1.24 us (2%)
    pallas_call x1, Pallas kernels, on_device(): pl.pallas_call(kernel, name='spliced', out_shape=(vmem((128, 256), BF16),...  66.5 us

profile of v7, /device:TPU:8, one launch (start us, length us, event | category | flops | bytes accessed | tf_op | source)
XLA Modules:
  0.0 68.3 jit_solution(2492064784331900058)
XLA Ops:
  0.6 66.5 %spliced.1 = (bf16[128,256]{1,0:T(8,128)(2,1)S(1)}, f32[32,128]{1,0:T(8,128)S(1)}) custom-call(bf16[32,224]{1,0:T(8,128)(2,1)} %hid_h.1, bf16[32,3584]{1,0:T(8,128)(2,1)} %resid_h.1, bf16[224,3584]{1,0:T(8,128)(2,1)} %d1_h.1, f32[28,128]{1,0:T(8,128)} %bitcast.11, bf16[3584,256]{1,0:T(8,128)(2,1)} %enc_h.1, f32[1,256]{1,0:T(1,128)} %bitcast.15, ...), custom_call_target="tpu_custom_call" | custom-call | flops 1000000000 | bytes 12000000 | tf_op jit(solution)/shard_map/spliced/pallas_call | solution.py:436
  67.1 0.6 copy.17
  67.7 0.6 copy.18
